TPU v7x, 32 devices: a whole 2x2x4 slice. The times are simulated.
32 devices in a mesh: tok: 4 (over z), tile: 4 (over y, core), pair: 2 (over x).
Axes of the slice: x: 2, y: 2, z: 4, core: 2. Of those that a mesh axis runs over, the one named last changes fastest.
Arguments:
- inputs: bfloat16 [4096, 4096], P(('tok', 'pair'), 'tile'), may hold values from -6 to 6
- output_grads: bfloat16 [4096, 4096], P(('tok', 'pair'), 'tile'), may hold values from -0.09375 to 0.09375
- statistics: float32 [16, 2, 1024, 1024], P('tile', 'pair', 'tok'), may hold values from -30 to 43008, as said below
Outputs:
- update: bfloat16 [16, 1024, 1024], P('tile', ('tok', 'pair'))
- new_statistics: float32 [16, 2, 1024, 1024], P('tile', 'pair', 'tok')
Inputs may be any that keep to these rules, and one draw needn't show every extreme that they name: `statistics`: for every block and factor the 1024 x 1024 matrix is symmetric and positive definite.
All inputs are finite; a program needn't handle non-finite values. Where the computation divides by a largest or mean magnitude, that divisor is 1e-20 or more.
Results may differ from a plain program's by a relative error of at most 0.00325.
The roundings to bfloat16 on the way count: a program that leaves them out, or rounds other values in their place, can miss the bound.
Values may be sent and summed in bfloat16 or wider, within the bound.
A program may use at most 128 MiB of HBM per device.

v0:
```python
import jax
import jax.numpy as jnp
from jax import lax
from jax.sharding import PartitionSpec as P

ITERS = 2


def swapped(shard, axis, stride):
    return lax.ppermute(shard, axis, [(i, i ^ 1 << stride) for i in range(lax.axis_size(axis))])


def product_bf(left_part, right_part):
    return jnp.einsum(
        "kab,kbc->kac", left_part, right_part, preferred_element_type=jnp.float32
    ).astype(jnp.bfloat16)


def per_device(inputs, output_grads, statistics):
    blocks = statistics.shape[0]
    state_rows = statistics.shape[2]
    matrix_order = statistics.shape[3]
    tile_count = lax.axis_size("tile")
    model_width = inputs.shape[1] * tile_count
    per_side = model_width // matrix_order
    tok_index = lax.axis_index("tok")
    pair_index = lax.axis_index("pair")
    shard_index = tok_index * lax.axis_size("pair") + pair_index
    devices_block = lax.axis_size("tok") * lax.axis_size("pair")
    out_rows = matrix_order // devices_block
    activations, cotangents = (
        lax.all_gather(inputs, "tile", axis=1, tiled=True),
        lax.all_gather(output_grads, "tile", axis=1, tiled=True),
    )
    first_block = lax.axis_index("tile") * blocks
    left_list = []
    right_list = []
    for offset in range(blocks):
        block_id = first_block + offset
        left_list.append(
            lax.dynamic_slice_in_dim(
                activations, block_id // per_side * matrix_order, matrix_order, 1
            )
        )
        right_list.append(
            lax.dynamic_slice_in_dim(
                cotangents, block_id % per_side * matrix_order, matrix_order, 1
            )
        )
    left_acts = jnp.stack(left_list)
    right_cots = jnp.stack(right_list)
    grad_share = lax.psum_scatter(
        jnp.einsum("ktr,ktc->rkc", left_acts, right_cots, preferred_element_type=jnp.float32),
        ("tok", "pair"),
        scatter_dimension=0,
        tiled=True,
    )
    gradient = lax.all_gather(grad_share.astype(jnp.bfloat16), ("tok", "pair"), axis=0, tiled=True)
    grad_sq = jnp.einsum("rkc,rkc->k", gradient, gradient, preferred_element_type=jnp.float32)
    by_rows = jnp.transpose(gradient, (1, 0, 2))
    by_cols = jnp.transpose(gradient, (1, 2, 0))
    factor_data = jnp.where(pair_index == 0, by_rows, by_cols)
    identity = jnp.eye(matrix_order, dtype=jnp.float32)
    row_start = tok_index * state_rows
    previous = lax.all_gather(statistics[:, 0], "tok", axis=1, tiled=True)
    product = jnp.einsum(
        "kac,kbc->kab", factor_data, factor_data, preferred_element_type=jnp.float32
    )
    updated = 0.9 * previous + 0.1 * product
    new_rows = lax.dynamic_slice_in_dim(updated, row_start, state_rows, 1)
    bound_max = jnp.max(jnp.sum(jnp.abs(updated), axis=2), axis=1)[:, None, None]
    iterate = ((updated + 0.1 * bound_max * identity) / (1.1 * bound_max)).astype(jnp.bfloat16)
    iterate = lax.optimization_barrier(iterate)
    root_whole = iterate
    for iteration in range(ITERS):
        factor = ((5.0 * identity - iterate.astype(jnp.float32)) / 4.0).astype(jnp.bfloat16)
        if iteration == 0:
            root_whole = factor
        else:
            root_whole = product_bf(root_whole, factor)
        if iteration + 1 < ITERS:
            square = product_bf(factor, factor)
            fourth = product_bf(square, square)
            iterate = lax.optimization_barrier(product_bf(fourth, iterate))
    partner = swapped(root_whole, "pair", 0)
    left_whole = jnp.where(pair_index == 0, root_whole, partner)
    right_whole = jnp.where(pair_index == 0, partner, root_whole)
    left_part = lax.dynamic_slice_in_dim(left_whole, shard_index * out_rows, out_rows, 1)
    left_mixed = jnp.einsum(
        "kqr,rkc->kqc", left_part, gradient, preferred_element_type=jnp.float32
    ).astype(jnp.bfloat16)
    raw_update = jnp.einsum(
        "kqc,kcd->kqd", left_mixed, right_whole, preferred_element_type=jnp.float32
    )
    local_sq = jnp.sum(raw_update * raw_update, axis=(1, 2))
    update_total = lax.psum(local_sq, ("tok", "pair"))
    graft_ratio = jnp.sqrt(grad_sq / (update_total + 1e-06))
    update = (raw_update * graft_ratio[:, None, None]).astype(jnp.bfloat16)
    return (update, new_rows[:, None])


def solution(mesh):
    placed = (
        P(("tok", "pair"), "tile"),
        P(("tok", "pair"), "tile"),
        P("tile", "pair", "tok", None),
    )
    return jax.shard_map(
        per_device,
        mesh=mesh,
        in_specs=placed,
        out_specs=(P("tile", ("tok", "pair"), None), P("tile", "pair", "tok", None)),
        check_vma=False,
    )
```

profile of v0, /device:TPU:8, one launch (start us, length us, event | category | flops | bytes accessed | tf_op | source)
XLA Modules:
  0.0 1117.4 jit_solution(6596002682313913743)
XLA Ops:
  7.2 0.0 all-gather.6.cloned.1.call-start
  7.2 0.7 all-gather.6.cloned.1.call-update
  7.9 0.0 all-gather.8.cloned.1.call-start
  7.9 0.7 all-gather.8.cloned.1.call-update
  8.6 0.0 reduce-scatter.2.cloned.1.call-start
  8.8 36.5 %all-gather.6.cloned.1.call-done = bf16[512,4096]{1,0:T(8,128)(2,1)} async-done(((bf16[512,1024]{1,0:T(8,128)(2,1)}), bf16[512,4096]{1,0:T(8,128)(2,1)}) %all-gather.6.cloned.1.call-update) | async-done | bytes 4194320 | tf_op jit(solution)/shard_map/all_gather | solution.py:33
  45.2 3.9 constant_dynamic-slice_fusion.3
  49.1 2.3 copy.24
  51.4 1.3 copy.25
  52.7 0.0 copy-start
  52.7 1.3 copy.26
  54.0 0.0 copy-start.1
  54.0 1.3 copy.27
  55.3 0.0 copy-start.2
  55.3 26.0 %all-gather.8.cloned.1.call-done = bf16[512,4096]{1,0:T(8,128)(2,1)} async-done(((bf16[512,1024]{1,0:T(8,128)(2,1)}), bf16[512,4096]{1,0:T(8,128)(2,1)}) %all-gather.8.cloned.1.call-update) | async-done | bytes 4194320 | tf_op jit(solution)/shard_map/all_gather | solution.py:32
  81.3 3.3 dynamic-slice_bitcast_fusion.4
  84.6 0.0 copy-done
  84.7 0.0 copy-done.1
  84.7 0.0 copy-done.2
  84.7 0.0 copy-done.3
  84.7 11.6 %convolution_bitcast_fusion = f32[1024,4,1024]{0,2,1:T(8,128)} fusion(bf16[1,512,1024]{1,2,0:T(8,128)(2,1)S(1)} %bitcast.40, bf16[1,512,1024]{1,2,0:T(8,128)(2,1)S(1)} %bitcast.39, bf16[1,512,1024]{1,2,0:T(8,128)(2,1)S(1)} %bitcast.38, bf16[1,512,1024]{1,2,0:T(8,128)(2,1)S(1)} %bitcast.37, bf16[1,512,1024]{2,1,0:T(8,128)(2,1)S(1)} %get-tuple-element.7, ...), kind=kOutput, calls=%fused_computation.7 | convolution fusion | flops 4307550208 | bytes 25165824 | tf_op jit(solution)/shard_map/ktr,ktc->rkc/dot_general | solution.py:53
  96.3 0.0 reduce-scatter.2.cloned.1.call-update
  96.3 0.0 all-gather.10.cloned.1.call-start
  96.3 281.4 %reduce-scatter.2.cloned.1.call-done = f32[128,4,1024]{0,2,1:T(8,128)} async-done(((f32[1024,4,1024]{0,2,1:T(8,128)}), f32[128,4,1024]{0,2,1:T(8,128)}) %reduce-scatter.2.cloned.1.call-update) | async-done | bytes 2097168 | tf_op jit(solution)/shard_map/reduce_scatter | solution.py:52
  377.7 2.7 convert_element_type.43
  380.4 0.0 all-gather.10.cloned.1.call-update
  380.5 0.2 all-gather.12.cloned.1.call-start
  380.7 5.4 copy.23
  386.1 0.0 all-gather.12.cloned.1.call-update
  386.1 2.5 fusion.32
  388.6 2.6 fusion.33
  391.1 113.5 %all-gather.10.cloned.1.call-done = bf16[1024,4,1024]{0,2,1:T(8,128)(2,1)} async-done(((bf16[128,4,1024]{0,2,1:T(8,128)(2,1)}), bf16[1024,4,1024]{0,2,1:T(8,128)(2,1)}) %all-gather.10.cloned.1.call-update) | async-done | bytes 8388624 | tf_op jit(solution)/shard_map/all_gather | solution.py:58
  504.6 11.4 %copy.28 = bf16[1024,4,1024]{2,0,1:T(8,128)(2,1)} copy(bf16[1024,4,1024]{0,2,1:T(8,128)(2,1)} %all-gather.10.cloned.1.call-done) | data formatting | bytes 16777216 | tf_op jit(solution)/shard_map/all_gather | solution.py:58
  516.1 274.5 %all-gather.12.cloned.1.call-done = f32[4,1,1024,1024]{2,3,0,1:T(8,128)} async-done(((f32[4,1,256,1024]{2,3,0,1:T(8,128)}), f32[4,1,1024,1024]{2,3,0,1:T(8,128)}) %all-gather.12.cloned.1.call-update) | async-done | bytes 16777232 | tf_op jit(solution)/shard_map/all_gather | solution.py:65
  790.6 25.0 %abs_reduce_fusion = (f32[4,1024]{1,0:T(4,128)S(1)}, f32[4,1024,1024]{1,2,0:T(8,128)}) fusion(bf16[1024,4,1024]{0,2,1:T(8,128)(2,1)} %all-gather.10.cloned.1.call-done, bf16[1024,4,1024]{2,0,1:T(8,128)(2,1)} %copy.28, pred[]{:T(512)S(6)} %eq.24, f32[4,1,1024,1024]{2,3,0,1:T(8,128)} %all-gather.12.cloned.1.call-done), kind=kOutput, calls=%fused_computation.6 | convolution fusion | flops 8615096320 | bytes 50348032 | tf_op jit(solution)/shard_map/kac,kbc->kab/dot_general | solution.py:66
  815.5 0.1 reduce_max.9
  815.7 10.9 divide_convert_fusion
  826.6 21.9 %fusion.17 = bf16[4,1024,1024]{2,1,0:T(8,128)(2,1)} fusion(bf16[4,1024,1024]{1,2,0:T(8,128)(2,1)} %divide_convert_fusion, f32[1024,1024]{0,1:T(8,128)} %fusion.33), kind=kOutput, calls=%fused_computation.23 | convolution fusion | flops 8606711808 | bytes 20971520 | tf_op jit(solution)/shard_map/kab,kbc->kac/dot_general | solution.py:14
  848.4 25.2 %fusion.13 = bf16[4,1024,1024]{1,2,0:T(8,128)(2,1)} fusion(bf16[4,1024,1024]{1,2,0:T(8,128)(2,1)} %divide_convert_fusion, bf16[4,1024,1024]{2,1,0:T(8,128)(2,1)} %fusion.17), kind=kOutput, calls=%fused_computation.21 | convolution fusion | flops 17188257792 | bytes 25165824 | tf_op jit(solution)/shard_map/kab,kbc->kac/dot_general | solution.py:14
  873.7 21.9 %fusion.16 = bf16[4,1024,1024]{2,1,0:T(8,128)(2,1)} fusion(bf16[4,1024,1024]{1,2,0:T(8,128)(2,1)} %fusion.13, f32[1024,1024]{0,1:T(8,128)} %fusion.33, bf16[4,1024,1024]{1,2,0:T(8,128)(2,1)} %divide_convert_fusion), kind=kOutput, calls=%fused_computation.22 | convolution fusion | flops 8627683328 | bytes 29360128 | tf_op jit(solution)/shard_map/kab,kbc->kac/dot_general | solution.py:14
  895.6 1.7 collective-permute-start
  897.3 4.5 dynamic-slice_bitcast_fusion
  901.7 5.3 copy.37
  907.1 5.8 fusion
  912.9 165.3 %collective-permute-done = bf16[4,1024,1024]{2,1,0:T(8,128)(2,1)} collective-permute-done((bf16[4,1024,1024]{2,1,0:T(8,128)(2,1)}, bf16[4,1024,1024]{2,1,0:T(8,128)(2,1)}, u32[]{:S(2)}, u32[]{:S(2)}) %collective-permute-start) | collective-permute-done | bytes 8388640 | tf_op jit(solution)/shard_map/ppermute | solution.py:10
  1078.2 12.5 %multiply_reduce_fusion = (f32[4]{0:T(128)S(1)}, f32[4,128,1024]{2,1,0:T(8,128)S(1)}) fusion(bf16[4,1024,1024]{2,1,0:T(8,128)(2,1)} %collective-permute-done, bf16[4,1024,1024]{2,1,0:T(8,128)(2,1)} %fusion.16, pred[]{:T(512)S(6)} %eq.24, bf16[1024,4,1024]{0,2,1:T(8,128)(2,1)} %all-gather.10.cloned.1.call-done, s32[]{:T(128)S(6)} %select_n.97), kind=kOutput, calls=%fused_computation.43 | convolution fusion | flops 2153775104 | bytes 29361680 | tf_op jit(solution)/shard_map/kqc,kcd->kqd/dot_general | solution.py:92
  1090.7 18.9 %psum.7 = f32[4]{0:T(128)S(1)} all-reduce(f32[4]{0:T(128)S(1)} %get-tuple-element.18), channel_id=1, replica_groups=mesh['tok'=4,'tile'=4,'pair'=2] {'tok','pair'}, use_global_device_ids=true, to_apply=%region_4.5 | all-reduce | flops 4 | bytes 32 | tf_op jit(solution)/shard_map/psum | solution.py:96
  1109.6 1.3 multiply_convert_fusion.7
  (3 shorter events, 0.0 us)
Async XLA Ops:
  7.2 38.1 %all-gather.6.cloned.1.call-start = ((), (), s32[]{:S(2)}) async-start(), calls=%async_computation.1 | async-start | bytes 5242880 | tf_op jit(solution)/shard_map/all_gather | solution.py:33
  7.9 73.4 %all-gather.8.cloned.1.call-start = ((), (), s32[]{:S(2)}) async-start(), calls=%async_computation.2 | async-start | bytes 5242880 | tf_op jit(solution)/shard_map/all_gather | solution.py:32
  8.6 369.1 %reduce-scatter.2.cloned.1.call-start = ((), (), s32[]{:S(2)}) async-start(), calls=%async_computation.3 | async-start | bytes 18874368 | tf_op jit(solution)/shard_map/reduce_scatter | solution.py:52
  52.7 32.0 %copy-start = (bf16[512,1024]{0,1:T(8,128)(2,1)S(1)}, bf16[512,1024]{0,1:T(8,128)(2,1)}, u32[]{:S(2)}) copy-start(bf16[512,1024]{0,1:T(8,128)(2,1)} %copy.24) | copy-start | bytes 3145732
  54.0 30.6 %copy-start.1 = (bf16[512,1024]{0,1:T(8,128)(2,1)S(1)}, bf16[512,1024]{0,1:T(8,128)(2,1)}, u32[]{:S(2)}) copy-start(bf16[512,1024]{0,1:T(8,128)(2,1)} %copy.25) | copy-start | bytes 3145732
  55.3 29.3 %copy-start.2 = (bf16[512,1024]{0,1:T(8,128)(2,1)S(1)}, bf16[512,1024]{0,1:T(8,128)(2,1)}, u32[]{:S(2)}) copy-start(bf16[512,1024]{0,1:T(8,128)(2,1)} %copy.26) | copy-start | bytes 3145732
  81.3 3.4 copy-start.3
  96.3 408.3 %all-gather.10.cloned.1.call-start = ((), (), s32[]{:S(2)}) async-start(), calls=%async_computation.4 | async-start | bytes 9437184 | tf_op jit(solution)/shard_map/all_gather | solution.py:58
  380.5 410.1 %all-gather.12.cloned.1.call-start = ((), (), s32[]{:S(2)}) async-start(), calls=%async_computation.5 | async-start | bytes 20971520 | tf_op jit(solution)/shard_map/all_gather | solution.py:65
  895.6 182.7 %collective-permute-start = (bf16[4,1024,1024]{2,1,0:T(8,128)(2,1)}, bf16[4,1024,1024]{2,1,0:T(8,128)(2,1)}, u32[]{:S(2)}, u32[]{:S(2)}) collective-permute-start(bf16[4,1024,1024]{2,1,0:T(8,128)(2,1)} %fusion.16), channel_id=1, source_target_pairs={{0,1},{1,0},{2,3},{3,2},{4,5},{5,4},{6,7},{7,6},{8,9},{9,8},{10,11... | collective-permute-start | bytes 25165832 | tf_op jit(solution)/shard_map/ppermute | solution.py:10
Sparse Core Ops, SparseCore 0:
  9.6 35.6 all-gather.5
  46.8 34.4 all-gather.7
  96.4 281.2 reduce-scatter.1
  380.6 124.0 all-gather.9
  506.7 283.8 all-gather.11
where the time goes:
time: 1120 us
  waiting for transfers between devices  899 us (80%)
  matrix products  118 us (11%)
  local copies, waits for them, and re-layouts  40.1 us (4%)
  other arithmetic  25.8 us (2%)
  blocking collectives  18.9 us (2%)
  between operations  13.9 us (1%)
    reduce_scatter x1, waiting for transfers between devices, per_device(): lax.psum_scatter(jnp.einsum('ktr,ktc->rkc', left_acts, right_cots, prefer...  281 us
    all_gather x1, waiting for transfers between devices, per_device(): previous = lax.all_gather(statistics[:, 0], 'tok', axis=1, tiled=True)  274 us
    ppermute x1, waiting for transfers between devices, swapped(): lax.ppermute(shard, axis, [(i, i ^ 1 << stride) for i in range(lax.axis_s...  165 us
    all_gather x1, waiting for transfers between devices, per_device(): lax.all_gather(grad_share.astype(jnp.bfloat16), ('tok', 'pair'), axis=0,...  113 us
    dot_general x3, matrix products, product_bf(): jnp.einsum('kab,kbc->kac', left_part, right_part, preferred_element_type=...  69 us
    all_gather x1, waiting for transfers between devices, per_device(): lax.all_gather(output_grads, 'tile', axis=1, tiled=True)  36.5 us
    all_gather x1, waiting for transfers between devices, per_device(): lax.all_gather(inputs, 'tile', axis=1, tiled=True)  26 us
    dot_general x1, matrix products, per_device(): jnp.einsum('kac,kbc->kab', factor_data, factor_data, preferred_element_ty...  25 us
  transfers between devices with their start and end apart: 6, of which 6 were waited for; matrix products, arithmetic and copies ran while one was open for 4% of the time, Pallas kernels for 0%

commit v1 on v0

--- a/solution.py
+++ b/solution.py
@@ -16,7 +16,7 @@
     ).astype(jnp.bfloat16)
 
 
-def per_device(inputs, output_grads, statistics):
+def general_plan(inputs, output_grads, statistics):
     blocks = statistics.shape[0]
     state_rows = statistics.shape[2]
     matrix_order = statistics.shape[3]
@@ -99,6 +99,110 @@
     return (update, new_rows[:, None])
 
 
+def dot_bf(left_part, right_part):
+    return jnp.dot(left_part, right_part, preferred_element_type=jnp.float32).astype(jnp.bfloat16)
+
+
+def exchange(pieces, axis):
+    size = lax.axis_size(axis)
+    index = lax.axis_index(axis)
+    result = pieces
+    for step in range(1, size):
+        piece = lax.dynamic_index_in_dim(pieces, index ^ step, 0, keepdims=True)
+        arrived = lax.ppermute(piece, axis, [(i, i ^ step) for i in range(size)])
+        result = lax.dynamic_update_slice_in_dim(result, arrived, index ^ step, 0)
+    return result
+
+
+def gather_cotangents(output_grads, tok_size):
+    tok_index = lax.axis_index("tok")
+    tile_index = lax.axis_index("tile")
+    quarters = output_grads.reshape(tok_size, -1, output_grads.shape[1])
+    held = jnp.zeros_like(quarters)
+    for step in range(tok_size):
+        pairs = [
+            (tok * tok_size + tile, tile * tok_size + (tok + step) % tok_size)
+            for tok in range(tok_size)
+            for tile in range(tok_size)
+        ]
+        piece = lax.dynamic_index_in_dim(quarters, (tok_index + step) % tok_size, 0, keepdims=True)
+        arrived = lax.ppermute(piece, ("tok", "tile"), pairs)
+        source = (tile_index + tok_size - step) % tok_size
+        held = lax.dynamic_update_slice_in_dim(held, arrived, source, 0)
+    return lax.all_gather(held, "tile", axis=0)
+
+
+def owner_plan(inputs, output_grads, statistics):
+    blocks, _, state_rows, order = statistics.shape
+    tok_index = lax.axis_index("tok")
+    pair_index = lax.axis_index("pair")
+    half = order // 2
+    cots = gather_cotangents(output_grads, blocks)
+    acts = lax.all_gather(inputs, "tok", axis=0)
+    cots = jnp.swapaxes(cots, 0, 1).reshape(-1, order)
+    acts = acts.reshape(-1, order)
+    previous = exchange(statistics[:, 0], "tok").reshape(order, order)
+
+    def share(which):
+        columns = lax.dynamic_slice_in_dim(acts, which * half, half, 1)
+        return lax.dot_general(
+            columns, cots, (((0,), (0,)), ((), ())), preferred_element_type=jnp.float32
+        )
+
+    theirs = swapped(share(1 - pair_index), "pair", 0)
+    mine = (share(pair_index) + theirs).astype(jnp.bfloat16)
+    other = swapped(mine, "pair", 0)
+    first = pair_index == 0
+    gradient = jnp.concatenate([jnp.where(first, mine, other), jnp.where(first, other, mine)], 0)
+    wide = gradient.astype(jnp.float32)
+    grad_sq = jnp.sum(wide * wide)
+    factor_data = jnp.where(first, gradient, gradient.T)
+    product = lax.dot_general(
+        factor_data, factor_data, (((1,), (1,)), ((), ())), preferred_element_type=jnp.float32
+    )
+    rows = exchange(product.astype(jnp.bfloat16).reshape(blocks, state_rows, order), "tok")
+    new_rows = 0.9 * statistics + 0.1 * rows[:, None].astype(jnp.float32)
+    updated = 0.9 * previous + 0.1 * product
+    identity = jnp.eye(order, dtype=jnp.float32)
+    bound_max = jnp.max(jnp.sum(jnp.abs(updated), axis=1))
+    iterate = ((updated + 0.1 * bound_max * identity) / (1.1 * bound_max)).astype(jnp.bfloat16)
+    iterate = lax.optimization_barrier(iterate)
+    root = iterate
+    for iteration in range(ITERS):
+        factor = ((5.0 * identity - iterate.astype(jnp.float32)) / 4.0).astype(jnp.bfloat16)
+        root = factor if iteration == 0 else dot_bf(root, factor)
+        if iteration + 1 < ITERS:
+            square = dot_bf(factor, factor)
+            fourth = dot_bf(square, square)
+            iterate = lax.optimization_barrier(dot_bf(fourth, iterate))
+    partner = swapped(root, "pair", 0)
+    left = jnp.where(first, root, partner)
+    right = jnp.where(first, partner, root)
+    left = left.reshape(blocks, 2, -1, order)
+    left_rows = lax.dynamic_index_in_dim(left, pair_index, 1, keepdims=False).reshape(-1, order)
+    left_mixed = dot_bf(left_rows, gradient)
+    raw = jnp.dot(left_mixed, right, preferred_element_type=jnp.float32)
+    local_sq = jnp.broadcast_to(jnp.sum(raw * raw), (8, 128))
+    update_sq = (local_sq + swapped(local_sq, "pair", 0))[0, 0]
+    update = (raw * jnp.sqrt(grad_sq / (update_sq + 1e-06))).astype(jnp.bfloat16)
+    return (exchange(update.reshape(blocks, -1, order), "tok"), new_rows)
+
+
+def per_device(inputs, output_grads, statistics):
+    blocks, _, _, order = statistics.shape
+    tok_size = lax.axis_size("tok")
+    owners = (
+        blocks == tok_size
+        and tok_size == lax.axis_size("tile")
+        and tok_size & (tok_size - 1) == 0
+        and lax.axis_size("pair") == 2
+        and inputs.shape[1] == order
+        and inputs.shape[0] % tok_size == 0
+    )
+    plan = owner_plan if owners else general_plan
+    return plan(inputs, output_grads, statistics)
+
+
 def solution(mesh):
     placed = (
         P(("tok", "pair"), "tile"),

time: 1120 us -> 418 us (0.37)
  waiting for transfers between devices: 899 us -> 286 us
  matrix products: 118 us -> 47.1 us
  starting transfers between devices: 2.08 us -> 21.5 us
  blocking collectives: 18.9 us -> 0 us
  local copies, waits for them, and re-layouts: 40.1 us -> 21.5 us
    all_gather x4 -> x2, waiting for transfers between devices: 450 us -> 59.6 us  [the longest x1 42 us: gather_cotangents(): return lax.all_gather(held, 'tile', axis=0)]
    reduce_scatter x1 -> x0, waiting for transfers between devices: 281 us -> none  [per_device(): lax.psum_scatter(jnp.einsum('ktr,ktc->rkc', left_acts, right_cots, prefer...]
    ppermute x0 -> x13, waiting for transfers between devices: none -> 146 us  [the longest x4 86.8 us: gather_cotangents(): arrived = lax.ppermute(piece, ('tok', 'tile'), pairs)]
    ppermute x1 -> x4, waiting for transfers between devices: 165 us -> 80 us  [swapped(): lax.ppermute(shard, axis, [(i, i ^ 1 << stride) for i in range(lax.axis_s...]
    dot_general x6 -> x7, matrix products: 118 us -> 47.1 us  [the longest x3 20.3 us: dot_bf(): jnp.dot(left_part, right_part, preferred_element_type=jnp.float32)]
    psum x1 -> x0, blocking collectives: 18.9 us -> none  [per_device(): update_total = lax.psum(local_sq, ('tok', 'pair'))]
    ppermute x0 -> x13, starting transfers between devices: none -> 17.3 us  [the longest x9 9.69 us: exchange(): arrived = lax.ppermute(piece, axis, [(i, i ^ step) for i in range(size)])]
    all_gather x1, local copies, waits for them, and re-layouts: 11.4 us -> 0.12 us  [gather_cotangents(): return lax.all_gather(held, 'tile', axis=0)]
  transfers between devices with their start and end apart: 6 -> 19, of which waited for: 6 -> 13; matrix products, arithmetic and copies ran while one was open for 4% -> 10% of each run, Pallas kernels for 0% -> 0%
where the time goes in v1:
time: 418 us; the launch traced here: 417 us
  waiting for transfers between devices  286 us (68%)
  matrix products  47.1 us (11%)
  other arithmetic  23.7 us (6%)
  starting transfers between devices  21.5 us (5%)
  local copies, waits for them, and re-layouts  21.5 us (5%)
  between operations  16.9 us (4%)
    ppermute x4, waiting for transfers between devices, gather_cotangents(): arrived = lax.ppermute(piece, ('tok', 'tile'), pairs)  86.8 us
    ppermute x4, waiting for transfers between devices, swapped(): lax.ppermute(shard, axis, [(i, i ^ 1 << stride) for i in range(lax.axis_s...  80 us
    ppermute x9, waiting for transfers between devices, exchange(): arrived = lax.ppermute(piece, axis, [(i, i ^ step) for i in range(size)])  59.1 us
    all_gather x1, waiting for transfers between devices, gather_cotangents(): return lax.all_gather(held, 'tile', axis=0)  42 us
    dot_general x3, matrix products, dot_bf(): jnp.dot(left_part, right_part, preferred_element_type=jnp.float32)  20.3 us
    all_gather x1, waiting for transfers between devices, owner_plan(): acts = lax.all_gather(inputs, 'tok', axis=0)  17.5 us
    dot_general x2, matrix products, share(): lax.dot_general(columns, cots, (((0,), (0,)), ((), ())), preferred_elemen...  12.3 us
    ppermute x9, starting transfers between devices, exchange(): arrived = lax.ppermute(piece, axis, [(i, i ^ step) for i in range(size)])  9.69 us
  transfers between devices with their start and end apart: 19, of which 13 were waited for; matrix products, arithmetic and copies ran while one was open for 10% of the time, Pallas kernels for 0%

profile of v1, /device:TPU:8, one launch (start us, length us, event | category | flops | bytes accessed | tf_op | source)
XLA Modules:
  0.0 417.0 jit_solution(10492827776960830938)
XLA Ops:
  7.2 0.7 all-gather.6.cloned.1.call-update
  8.0 1.3 constant_dynamic-slice_fusion.7
  9.3 1.9 collective-permute-start.3
  11.2 4.0 collective-permute-start.4
  15.2 1.2 collective-permute-start.5
  17.1 12.8 %collective-permute-done.4 = bf16[1,128,1024]{2,1,0:T(8,128)(2,1)S(1)} collective-permute-done((bf16[1,128,1024]{2,1,0:T(8,128)(2,1)S(1)}, bf16[1,128,1024]{2,1,0:T(8,128)(2,1)S(1)}, u32[]{:S(2)}, u32[]{:S(2)}) %collective-permute-start.4) | collective-permute-done | bytes 262176 | tf_op jit(solution)/shard_map/ppermute | solution.py:129
  29.9 74.0 %collective-permute-done.5 = bf16[1,128,1024]{2,1,0:T(8,128)(2,1)S(1)} collective-permute-done((bf16[1,128,1024]{2,1,0:T(8,128)(2,1)S(1)}, bf16[1,128,1024]{2,1,0:T(8,128)(2,1)S(1)}, u32[]{:S(2)}, u32[]{:S(2)}) %collective-permute-start.5) | collective-permute-done | bytes 262176 | tf_op jit(solution)/shard_map/ppermute | solution.py:129
  104.0 1.0 copy-done.2
  105.0 17.5 %all-gather.6.cloned.1.call-done = bf16[2048,1024]{1,0:T(8,128)(2,1)} async-done(((bf16[512,1024]{1,0:T(8,128)(2,1)}), bf16[2048,1024]{1,0:T(8,128)(2,1)}) %all-gather.6.cloned.1.call-update) | async-done | bytes 4194320 | tf_op jit(solution)/shard_map/all_gather | solution.py:141
  122.5 42.0 %all-gather.4.cloned.1.call-done = bf16[4,4,128,1024]{3,2,0,1:T(8,128)(2,1)} async-done(((bf16[1,4,128,1024]{3,2,0,1:T(8,128)(2,1)}), bf16[4,4,128,1024]{3,2,0,1:T(8,128)(2,1)}) %all-gather.4.cloned.1.call-update) | async-done | bytes 4194320 | tf_op jit(solution)/shard_map/all_gather | solution.py:132
  164.5 6.5 %fusion.16 = f32[512,1024]{1,0:T(8,128)} fusion(bf16[2048,1024]{1,0:T(8,128)(2,1)} %bitcast.63, bf16[2048,1024]{1,0:T(8,128)(2,1)} %all-gather.6.cloned.1.call-done, s32[]{:T(128)S(6)} %select_n.146), kind=kOutput, calls=%fused_computation.28 | convolution fusion | flops 2147483648 | bytes 8388612 | tf_op jit(solution)/shard_map/dot_general | solution.py:148
  171.0 1.5 collective-permute-start.7
  172.5 3.7 dynamic-slice_bitcast_fusion
  176.7 2.4 collective-permute-start.1
  179.6 39.5 %collective-permute-done.7 = f32[512,1024]{1,0:T(8,128)} collective-permute-done((f32[512,1024]{1,0:T(8,128)}, f32[512,1024]{1,0:T(8,128)}, u32[]{:S(2)}, u32[]{:S(2)}) %collective-permute-start.7) | collective-permute-done | bytes 2097184 | tf_op jit(solution)/shard_map/ppermute | solution.py:10
  219.1 5.8 %add_convert_fusion = bf16[512,1024]{1,0:T(8,128)(2,1)S(1)} fusion(f32[512,1024]{1,0:T(8,128)} %collective-permute-done.7, bf16[2048,1024]{1,0:T(8,128)(2,1)} %bitcast.64, bf16[2048,1024]{1,0:T(8,128)(2,1)} %all-gather.6.cloned.1.call-done, s32[]{:T(128)S(6)} %select_n.129), kind=kOutput, calls=%fused_computation.27 | convolution fusion | flops 2148532224 | bytes 9437188 | tf_op jit(solution)/shard_map/dot_general | solution.py:148
  224.9 1.5 collective-permute-start.8
  226.5 2.2 copy.12
  228.7 1.3 constant_dynamic-update-slice_fusion.5
  230.0 18.0 %collective-permute-done.1 = f32[1,256,1024]{2,1,0:T(8,128)S(1)} collective-permute-done((f32[1,256,1024]{2,1,0:T(8,128)}, f32[1,256,1024]{2,1,0:T(8,128)S(1)}, u32[]{:S(2)}, u32[]{:S(2)}) %collective-permute-start.1) | collective-permute-done | bytes 1048608 | tf_op jit(solution)/shard_map/ppermute | solution.py:112
  248.1 22.0 %collective-permute-done.2 = f32[1,256,1024]{2,1,0:T(8,128)S(1)} collective-permute-done((f32[1,256,1024]{2,1,0:T(8,128)}, f32[1,256,1024]{2,1,0:T(8,128)S(1)}, u32[]{:S(2)}, u32[]{:S(2)}) %collective-permute-start.2) | collective-permute-done | bytes 1048608 | tf_op jit(solution)/shard_map/ppermute | solution.py:112
  270.2 2.5 broadcast_multiply_fusion
  272.7 1.4 broadcast_select_fusion.2
  274.0 1.6 pad_maximum_fusion
  275.7 4.0 copy.10
  279.6 7.9 %abs_reduce_fusion = (f32[1024]{0:T(1024)S(1)}, f32[1024,1024]{1,0:T(8,128)}) fusion(f32[4,256,1024]{2,1,0:T(8,128)} %broadcast_multiply_fusion, bf16[1024,1024]{0,1:T(8,128)(2,1)} %copy.10, pred[]{:T(512)S(6)} %eq.19, bf16[512,1024]{1,0:T(8,128)(2,1)S(1)} %get-tuple-element.11, bf16[512,1024]{1,0:T(8,128)(2,1)S(1)} %get-tuple-element.10), kind=kOutput, calls=%fused_computation.10 | convolution fusion | flops 2156919808 | bytes 12587009 | tf_op jit(solution)/shard_map/dot_general | solution.py:160
  289.5 7.4 %fusion.48 = (bf16[1024,1024]{1,0:T(8,128)(2,1)S(1)}, bf16[1024,1024]{1,0:T(8,128)(2,1)}) fusion(f32[1024,1024]{1,0:T(8,128)} %get-tuple-element.20, f32[]{:T(128)S(6)} %mul_shard_map.3, f32[]{:T(128)S(6)} %mul.68, f32[4,256,1024]{2,1,0:T(8,128)} %broadcast_multiply_fusion), kind=kLoop, calls=%fused_computation.78 | loop fusion | flops 8388608 | bytes 12582920 | tf_op jit(solution)/shard_map/convert_element_type | solution.py:163
  296.9 11.7 %fusion.13 = bf16[1024,1024]{1,0:T(8,128)(2,1)} fusion(bf16[1024,1024]{1,0:T(8,128)(2,1)} %get-tuple-element.3), kind=kOutput, calls=%fused_computation.24 | convolution fusion | flops 4302307328 | bytes 4194304 | tf_op jit(solution)/shard_map/dot_general | solution.py:103
  308.6 4.7 %fusion.22 = bf16[1024,1024]{1,0:T(8,128)(2,1)S(1)} fusion(bf16[1024,1024]{1,0:T(8,128)(2,1)} %get-tuple-element.3, bf16[1024,1024]{1,0:T(8,128)(2,1)} %fusion.13), kind=kOutput, calls=%fused_computation.36 | convolution fusion | flops 2148532224 | bytes 6291456 | tf_op jit(solution)/shard_map/dot_general | solution.py:103
  313.3 4.0 fusion.25
  317.8 1.2 constant_dynamic-slice_fusion
  319.0 2.9 collective-permute-start.15
  322.5 2.9 multiply_reduce_fusion
  325.4 38.5 %collective-permute-done.9 = bf16[1024,1024]{1,0:T(8,128)(2,1)} collective-permute-done((bf16[1024,1024]{1,0:T(8,128)(2,1)}, bf16[1024,1024]{1,0:T(8,128)(2,1)}, u32[]{:S(2)}, u32[]{:S(2)}) %collective-permute-start.9) | collective-permute-done | bytes 2097184 | tf_op jit(solution)/shard_map/ppermute | solution.py:10
  363.9 1.8 broadcast_select_fusion
  365.7 1.0 constant_dynamic-slice_fusion.6
  366.8 6.6 %multiply_reduce_fusion.1 = (f32[]{:T(128)}, f32[512,1024]{1,0:T(8,128)}) fusion(bf16[1024,1024]{1,0:T(8,128)(2,1)} %collective-permute-done.9, bf16[1024,1024]{1,0:T(8,128)(2,1)} %fusion.25, pred[]{:T(512)S(6)} %eq.19, bf16[512,1024]{1,0:T(8,128)(2,1)} %bitcast.62, bf16[512,1024]{1,0:T(8,128)(2,1)} %copy-done.1, bf16[512,1024]{1,0:T(8,128)(2,1)S(1)} %get-tuple-element.10), kind=kOutput, calls=%fused_computation.19 | convolution fusion | flops 2154299392 | bytes 9437189 | tf_op jit(solution)/shard_map/dot_general | solution.py:184
  374.6 1.1 bitcast_dynamic-update-slice_fusion.2
  375.7 2.0 collective-permute-done.10
  380.1 2.0 multiply_convert_fusion
  382.2 1.1 bitcast_dynamic-update-slice_fusion.1
  383.3 1.1 bitcast_dynamic-update-slice_fusion
  384.4 4.8 %collective-permute-done.11 = bf16[1,128,1024]{2,1,0:T(8,128)(2,1)S(1)} collective-permute-done((bf16[1,128,1024]{2,1,0:T(8,128)(2,1)S(1)}, bf16[1,128,1024]{2,1,0:T(8,128)(2,1)S(1)}, u32[]{:S(2)}, u32[]{:S(2)}) %collective-permute-start.11) | collective-permute-done | bytes 262176 | tf_op jit(solution)/shard_map/ppermute | solution.py:112
  389.2 2.0 collective-permute-start.12
  391.9 2.9 multiply_add_fusion
  394.8 9.8 %collective-permute-done.12 = bf16[1,128,1024]{2,1,0:T(8,128)(2,1)S(1)} collective-permute-done((bf16[1,128,1024]{2,1,0:T(8,128)(2,1)S(1)}, bf16[1,128,1024]{2,1,0:T(8,128)(2,1)S(1)}, u32[]{:S(2)}, u32[]{:S(2)}) %collective-permute-start.12) | collective-permute-done | bytes 262176 | tf_op jit(solution)/shard_map/ppermute | solution.py:112
  404.5 4.6 %collective-permute-done.13 = bf16[1,128,1024]{2,1,0:T(8,128)(2,1)S(1)} collective-permute-done((bf16[1,128,1024]{2,1,0:T(8,128)(2,1)S(1)}, bf16[1,128,1024]{2,1,0:T(8,128)(2,1)S(1)}, u32[]{:S(2)}, u32[]{:S(2)}) %collective-permute-start.13) | collective-permute-done | bytes 262176 | tf_op jit(solution)/shard_map/ppermute | solution.py:112
  409.2 1.0 copy-done.3
  (42 shorter events, 7.2 us)
Async XLA Ops:
  7.2 115.3 %all-gather.6.cloned.1.call-start = ((), (), s32[]{:S(2)}) async-start(), calls=%async_computation.1 | async-start | bytes 5242880 | tf_op jit(solution)/shard_map/all_gather | solution.py:141
  7.9 156.6 %all-gather.4.cloned.1.call-start = ((), (), s32[]{:S(2)}) async-start(), calls=%async_computation | async-start | bytes 5242880 | tf_op jit(solution)/shard_map/all_gather | solution.py:132
  9.3 7.7 %collective-permute-start.3 = (bf16[1,128,1024]{2,1,0:T(8,128)(2,1)S(1)}, bf16[1,128,1024]{2,1,0:T(8,128)(2,1)S(1)}, u32[]{:S(2)}, u32[]{:S(2)}) collective-permute-start(bf16[1,128,1024]{2,1,0:T(8,128)(2,1)S(1)} %get-tuple-element.18), channel_id=1, source_target_pairs={{0,0},{2,8},{4,16},{6,24},{8,2},{10,10},{12,18},{14,26},{16,4},{18... | collective-permute-start | bytes 786440 | tf_op jit(solution)/shard_map/ppermute | solution.py:129
  11.2 18.7 %collective-permute-start.4 = (bf16[1,128,1024]{2,1,0:T(8,128)(2,1)S(1)}, bf16[1,128,1024]{2,1,0:T(8,128)(2,1)S(1)}, u32[]{:S(2)}, u32[]{:S(2)}) collective-permute-start(bf16[1,128,1024]{2,1,0:T(8,128)(2,1)S(1)} %get-tuple-element.17), channel_id=1, source_target_pairs={{0,2},{2,10},{4,18},{6,26},{8,4},{10,12},{12,20},{14,28},{16,6},{1... | collective-permute-start | bytes 786440 | tf_op jit(solution)/shard_map/ppermute | solution.py:129
  15.2 88.7 %collective-permute-start.5 = (bf16[1,128,1024]{2,1,0:T(8,128)(2,1)S(1)}, bf16[1,128,1024]{2,1,0:T(8,128)(2,1)S(1)}, u32[]{:S(2)}, u32[]{:S(2)}) collective-permute-start(bf16[1,128,1024]{2,1,0:T(8,128)(2,1)S(1)} %get-tuple-element.16), channel_id=1, source_target_pairs={{0,4},{2,12},{4,20},{6,28},{8,6},{10,14},{12,22},{14,30},{16,0},{1... | collective-permute-start | bytes 786440 | tf_op jit(solution)/shard_map/ppermute | solution.py:129
  16.4 87.6 %collective-permute-start.6 = (bf16[1,128,1024]{2,1,0:T(8,128)(2,1)S(1)}, bf16[1,128,1024]{2,1,0:T(8,128)(2,1)S(1)}, u32[]{:S(2)}, u32[]{:S(2)}) collective-permute-start(bf16[1,128,1024]{2,1,0:T(8,128)(2,1)S(1)} %get-tuple-element.15), channel_id=1, source_target_pairs={{0,6},{2,14},{4,22},{6,30},{8,0},{10,8},{12,16},{14,24},{16,2},{18... | collective-permute-start | bytes 786440 | tf_op jit(solution)/shard_map/ppermute | solution.py:129
  104.0 1.0 copy-start.2
  171.0 48.1 %collective-permute-start.7 = (f32[512,1024]{1,0:T(8,128)}, f32[512,1024]{1,0:T(8,128)}, u32[]{:S(2)}, u32[]{:S(2)}) collective-permute-start(f32[512,1024]{1,0:T(8,128)} %fusion.16), channel_id=1, source_target_pairs={{0,1},{1,0},{2,3},{3,2},{4,5},{5,4},{6,7},{7,6},{8,9},{9,8},{10,11... | collective-permute-start | bytes 6291464 | tf_op jit(solution)/shard_map/ppermute | solution.py:10
  176.2 52.5 %collective-permute-start = (f32[1,256,1024]{2,1,0:T(8,128)}, f32[1,256,1024]{2,1,0:T(8,128)}, u32[]{:S(2)}, u32[]{:S(2)}) collective-permute-start(f32[1,256,1024]{2,1,0:T(8,128)} %get-tuple-element.6), channel_id=1, source_target_pairs={{0,8},{8,0},{16,24},{24,16},{1,9},{9,1},{17,25},{25,17},{2,10},{10... | collective-permute-start | bytes 3145736 | tf_op jit(solution)/shard_map/ppermute | solution.py:112
  176.7 71.3 %collective-permute-start.1 = (f32[1,256,1024]{2,1,0:T(8,128)}, f32[1,256,1024]{2,1,0:T(8,128)S(1)}, u32[]{:S(2)}, u32[]{:S(2)}) collective-permute-start(f32[1,256,1024]{2,1,0:T(8,128)} %get-tuple-element.5), channel_id=1, source_target_pairs={{0,16},{8,24},{16,0},{24,8},{1,17},{9,25},{17,1},{25,9},{2,18},{10... | collective-permute-start | bytes 3145736 | tf_op jit(solution)/shard_map/ppermute | solution.py:112
  179.1 90.9 %collective-permute-start.2 = (f32[1,256,1024]{2,1,0:T(8,128)}, f32[1,256,1024]{2,1,0:T(8,128)S(1)}, u32[]{:S(2)}, u32[]{:S(2)}) collective-permute-start(f32[1,256,1024]{2,1,0:T(8,128)} %get-tuple-element.4), channel_id=1, source_target_pairs={{0,24},{8,16},{16,8},{24,0},{1,25},{9,17},{17,9},{25,1},{2,26},{10... | collective-permute-start | bytes 3145736 | tf_op jit(solution)/shard_map/ppermute | solution.py:112
  224.9 47.7 %collective-permute-start.8 = (bf16[512,1024]{1,0:T(8,128)(2,1)S(1)}, bf16[512,1024]{1,0:T(8,128)(2,1)}, u32[]{:S(2)}, u32[]{:S(2)}) collective-permute-start(bf16[512,1024]{1,0:T(8,128)(2,1)S(1)} %add_convert_fusion), channel_id=1, source_target_pairs={{0,1},{1,0},{2,3},{3,2},{4,5},{5,4},{6,7},{7,6},{8,9},{9,8},{10,11... | collective-permute-start | bytes 3145736 | tf_op jit(solution)/shard_map/ppermute | solution.py:10
  274.0 5.6 %copy-start.1 = (bf16[512,1024]{1,0:T(8,128)(2,1)}, bf16[512,1024]{1,0:T(8,128)(2,1)S(1)}, u32[]{:S(2)}) copy-start(bf16[512,1024]{1,0:T(8,128)(2,1)S(1)} %get-tuple-element.11) | copy-start | bytes 3145732
  308.6 4.7 %copy-start.4 = (bf16[1024,1024]{1,0:T(8,128)(2,1)S(1)}, bf16[1024,1024]{1,0:T(8,128)(2,1)}, u32[]{:S(2)}) copy-start(bf16[1024,1024]{1,0:T(8,128)(2,1)} %get-tuple-element.3) | copy-start | bytes 6291460
  317.2 46.7 %collective-permute-start.9 = (bf16[1024,1024]{1,0:T(8,128)(2,1)}, bf16[1024,1024]{1,0:T(8,128)(2,1)}, u32[]{:S(2)}, u32[]{:S(2)}) collective-permute-start(bf16[1024,1024]{1,0:T(8,128)(2,1)} %fusion.25), channel_id=1, source_target_pairs={{0,1},{1,0},{2,3},{3,2},{4,5},{5,4},{6,7},{7,6},{8,9},{9,8},{10,11... | collective-permute-start | bytes 6291464 | tf_op jit(solution)/shard_map/ppermute | solution.py:10
  319.0 55.6 %collective-permute-start.14 = (bf16[1,256,1024]{2,1,0:T(8,128)(2,1)}, bf16[1,256,1024]{2,1,0:T(8,128)(2,1)}, u32[]{:S(2)}, u32[]{:S(2)}) collective-permute-start(bf16[1,256,1024]{2,1,0:T(8,128)(2,1)} %get-tuple-element.9), channel_id=1, source_target_pairs={{0,8},{8,0},{16,24},{24,16},{1,9},{9,1},{17,25},{25,17},{2,10},{10... | collective-permute-start | bytes 1572872 | tf_op jit(solution)/shard_map/ppermute | solution.py:112
  319.0 63.2 %collective-permute-start.15 = (bf16[1,256,1024]{2,1,0:T(8,128)(2,1)}, bf16[1,256,1024]{2,1,0:T(8,128)(2,1)}, u32[]{:S(2)}, u32[]{:S(2)}) collective-permute-start(bf16[1,256,1024]{2,1,0:T(8,128)(2,1)} %get-tuple-element.8), channel_id=1, source_target_pairs={{0,16},{8,24},{16,0},{24,8},{1,17},{9,25},{17,1},{25,9},{2,18},{10... | collective-permute-start | bytes 1572872 | tf_op jit(solution)/shard_map/ppermute | solution.py:112
  321.9 61.3 %collective-permute-start.16 = (bf16[1,256,1024]{2,1,0:T(8,128)(2,1)}, bf16[1,256,1024]{2,1,0:T(8,128)(2,1)}, u32[]{:S(2)}, u32[]{:S(2)}) collective-permute-start(bf16[1,256,1024]{2,1,0:T(8,128)(2,1)} %get-tuple-element.7), channel_id=1, source_target_pairs={{0,24},{8,16},{16,8},{24,0},{1,25},{9,17},{17,9},{25,1},{2,26},{10... | collective-permute-start | bytes 1572872 | tf_op jit(solution)/shard_map/ppermute | solution.py:112
  374.0 3.7 collective-permute-start.10
  380.0 11.8 %copy-start = (f32[4,1,256,1024]{3,2,1,0:T(8,128)S(1)}, f32[4,1,256,1024]{3,2,1,0:T(8,128)}, u32[]{:S(2)}) copy-start(f32[4,1,256,1024]{3,2,1,0:T(8,128)} %param.5) | copy-start | bytes 12582916
  382.1 7.1 %collective-permute-start.11 = (bf16[1,128,1024]{2,1,0:T(8,128)(2,1)S(1)}, bf16[1,128,1024]{2,1,0:T(8,128)(2,1)S(1)}, u32[]{:S(2)}, u32[]{:S(2)}) collective-permute-start(bf16[1,128,1024]{2,1,0:T(8,128)(2,1)S(1)} %constant_dynamic-slice_fusion.5), channel_id=1, source_target_pairs={{0,8},{8,0},{16,24},{24,16},{1,9},{9,1},{17,25},{25,17},{2,10},{10... | collective-permute-start | bytes 786440 | tf_op jit(solution)/shard_map/ppermute | solution.py:112
  389.2 15.3 %collective-permute-start.12 = (bf16[1,128,1024]{2,1,0:T(8,128)(2,1)S(1)}, bf16[1,128,1024]{2,1,0:T(8,128)(2,1)S(1)}, u32[]{:S(2)}, u32[]{:S(2)}) collective-permute-start(bf16[1,128,1024]{2,1,0:T(8,128)(2,1)S(1)} %get-tuple-element.13), channel_id=1, source_target_pairs={{0,16},{8,24},{16,0},{24,8},{1,17},{9,25},{17,1},{25,9},{2,18},{10... | collective-permute-start | bytes 786440 | tf_op jit(solution)/shard_map/ppermute | solution.py:112
  391.2 17.9 %collective-permute-start.13 = (bf16[1,128,1024]{2,1,0:T(8,128)(2,1)S(1)}, bf16[1,128,1024]{2,1,0:T(8,128)(2,1)S(1)}, u32[]{:S(2)}, u32[]{:S(2)}) collective-permute-start(bf16[1,128,1024]{2,1,0:T(8,128)(2,1)S(1)} %get-tuple-element.12), channel_id=1, source_target_pairs={{0,24},{8,16},{16,8},{24,0},{1,25},{9,17},{17,9},{25,1},{2,26},{10... | collective-permute-start | bytes 786440 | tf_op jit(solution)/shard_map/ppermute | solution.py:112
  409.2 1.0 copy-start.3
Sparse Core Ops, SparseCore 0:
  9.6 112.8 all-gather.5
  124.6 39.8 all-gather.3

commit v2 on v1

--- a/solution.py
+++ b/solution.py
@@ -114,7 +114,7 @@
     return result
 
 
-def gather_cotangents(output_grads, tok_size):
+def cotangent_quarter(output_grads, tok_size):
     tok_index = lax.axis_index("tok")
     tile_index = lax.axis_index("tile")
     quarters = output_grads.reshape(tok_size, -1, output_grads.shape[1])
@@ -129,7 +129,17 @@
         arrived = lax.ppermute(piece, ("tok", "tile"), pairs)
         source = (tile_index + tok_size - step) % tok_size
         held = lax.dynamic_update_slice_in_dim(held, arrived, source, 0)
-    return lax.all_gather(held, "tile", axis=0)
+    return held
+
+
+def spread_over_tile(piece):
+    index = lax.axis_index("tile")
+    held = [(index, piece)]
+    bit = lax.axis_size("tile").bit_length() - 2
+    while bit >= 0:
+        held += [(which ^ (1 << bit), swapped(part, "tile", bit)) for which, part in held]
+        bit -= 1
+    return held
 
 
 def owner_plan(inputs, output_grads, statistics):
@@ -137,20 +147,35 @@
     tok_index = lax.axis_index("tok")
     pair_index = lax.axis_index("pair")
     half = order // 2
-    cots = gather_cotangents(output_grads, blocks)
-    acts = lax.all_gather(inputs, "tok", axis=0)
-    cots = jnp.swapaxes(cots, 0, 1).reshape(-1, order)
-    acts = acts.reshape(-1, order)
-    previous = exchange(statistics[:, 0], "tok").reshape(order, order)
-
-    def share(which):
-        columns = lax.dynamic_slice_in_dim(acts, which * half, half, 1)
-        return lax.dot_general(
-            columns, cots, (((0,), (0,)), ((), ())), preferred_element_type=jnp.float32
-        )
-
-    theirs = swapped(share(1 - pair_index), "pair", 0)
-    mine = (share(pair_index) + theirs).astype(jnp.bfloat16)
+    quarter = inputs.shape[0] // blocks
+    held = cotangent_quarter(output_grads, blocks)
+    acts_mine = lax.dynamic_slice_in_dim(inputs, pair_index * half, half, 1)
+    acts_given = lax.dynamic_slice_in_dim(inputs, (1 - pair_index) * half, half, 1)
+    acts = jnp.concatenate([acts_mine, swapped(acts_given, "pair", 0)], 0)
+    acts, held = lax.optimization_barrier((acts, held))
+    acts = lax.all_gather(acts, "tok", axis=0, tiled=True)
+    cots = jnp.zeros((blocks, 2, blocks, quarter, order), output_grads.dtype)
+    for side, part in enumerate((held, swapped(held, "pair", 0))):
+        for which, piece in spread_over_tile(part):
+            cots = lax.dynamic_update_slice(cots, piece[:, None, None], (0, side, which, 0, 0))
+    cots = cots.reshape(-1, order)
+
+    rows_index = tok_index * state_rows
+    local_eye = jnp.arange(order)[None, :] == rows_index + jnp.arange(state_rows)[:, None]
+    diagonal = jnp.sum(jnp.where(local_eye[None], statistics[:, 0], 0.0), axis=1)
+    remainder = diagonal - lax.reduce_precision(diagonal, 8, 7)
+    extra = jnp.broadcast_to(remainder[:, None], (blocks, 16, order))
+    pieces = jnp.concatenate([statistics[:, 0], extra], 1).astype(jnp.bfloat16)
+    pieces, acts = lax.optimization_barrier((pieces, acts))
+    arrived = exchange(pieces, "tok")
+    identity = jnp.eye(order, dtype=jnp.float32)
+    lost = jnp.sum(arrived[:, state_rows].astype(jnp.float32), axis=0)
+    previous = arrived[:, :state_rows].reshape(order, order).astype(jnp.float32)
+    previous = previous + identity * lost
+
+    mine = lax.dot_general(
+        acts, cots, (((0,), (0,)), ((), ())), preferred_element_type=jnp.float32
+    ).astype(jnp.bfloat16)
     other = swapped(mine, "pair", 0)
     first = pair_index == 0
     gradient = jnp.concatenate([jnp.where(first, mine, other), jnp.where(first, other, mine)], 0)
@@ -161,7 +186,6 @@
         factor_data, factor_data, (((1,), (1,)), ((), ())), preferred_element_type=jnp.float32
     )
     rows = exchange(product.astype(jnp.bfloat16).reshape(blocks, state_rows, order), "tok")
-    new_rows = 0.9 * statistics + 0.1 * rows[:, None].astype(jnp.float32)
     updated = 0.9 * previous + 0.1 * product
     identity = jnp.eye(order, dtype=jnp.float32)
     bound_max = jnp.max(jnp.sum(jnp.abs(updated), axis=1))
@@ -175,6 +199,7 @@
             square = dot_bf(factor, factor)
             fourth = dot_bf(square, square)
             iterate = lax.optimization_barrier(dot_bf(fourth, iterate))
+    root, rows = lax.optimization_barrier((root, rows))
     partner = swapped(root, "pair", 0)
     left = jnp.where(first, root, partner)
     right = jnp.where(first, partner, root)
@@ -185,6 +210,7 @@
     local_sq = jnp.broadcast_to(jnp.sum(raw * raw), (8, 128))
     update_sq = (local_sq + swapped(local_sq, "pair", 0))[0, 0]
     update = (raw * jnp.sqrt(grad_sq / (update_sq + 1e-06))).astype(jnp.bfloat16)
+    new_rows = 0.9 * statistics + 0.1 * rows[:, None].astype(jnp.float32)
     return (exchange(update.reshape(blocks, -1, order), "tok"), new_rows)
 
 

time: 418 us -> 406 us (0.971)
  waiting for transfers between devices: 286 us -> 248 us
  local copies, waits for them, and re-layouts: 21.5 us -> 41.1 us
  starting transfers between devices: 21.5 us -> 30.8 us
  matrix products: 47.1 us -> 40.4 us
    ppermute x9, waiting for transfers between devices: 59.1 us -> 116 us  [exchange(): arrived = lax.ppermute(piece, axis, [(i, i ^ step) for i in range(size)])]
    ppermute x4, waiting for transfers between devices: 86.8 us -> 32.4 us  [cotangent_quarter(): arrived = lax.ppermute(piece, ('tok', 'tile'), pairs)]
    all_gather x2 -> x1, waiting for transfers between devices: 59.6 us -> 19.8 us  [owner_plan(): acts = lax.all_gather(acts, 'tok', axis=0, tiled=True)]
    dynamic_update_slice x4 -> x12, local copies, waits for them, and re-layouts: 0.09 us -> 18.3 us  [the longest x8 14.4 us: owner_plan(): lax.dynamic_update_slice(cots, piece[:, None, None], (0, side, which, 0, 0))]
    ppermute x4 -> x11, starting transfers between devices: 4.17 us -> 12 us  [swapped(): lax.ppermute(shard, axis, [(i, i ^ 1 << stride) for i in range(lax.axis_s...]
    broadcast_in_dim x0 -> x3, local copies, waits for them, and re-layouts: none -> 4.48 us  [the longest x1 4.34 us: owner_plan(): cots = jnp.zeros((blocks, 2, blocks, quarter, order), output_grads.dtype)]
    dot_general x2 -> x1, matrix products: 12.3 us -> 9.16 us  [owner_plan(): lax.dot_general(acts, cots, (((0,), (0,)), ((), ())), preferred_element_t...]
    ppermute x4 -> x11, waiting for transfers between devices: 80 us -> 79.8 us  [swapped(): lax.ppermute(shard, axis, [(i, i ^ 1 << stride) for i in range(lax.axis_s...]
  transfers between devices with their start and end apart: 19 -> 25, of which waited for: 13 -> 17; matrix products, arithmetic and copies ran while one was open for 10% -> 17% of each run, Pallas kernels for 0% -> 0%
where the time goes in v2:
time: 406 us; the launch traced here: 405 us
  waiting for transfers between devices  248 us (61%)
  local copies, waits for them, and re-layouts  41.1 us (10%)
  matrix products  40.4 us (10%)
  starting transfers between devices  30.8 us (8%)
  other arithmetic  27.7 us (7%)
  between operations  17.1 us (4%)
    ppermute x9, waiting for transfers between devices, exchange(): arrived = lax.ppermute(piece, axis, [(i, i ^ step) for i in range(size)])  116 us
    ppermute x11, waiting for transfers between devices, swapped(): lax.ppermute(shard, axis, [(i, i ^ 1 << stride) for i in range(lax.axis_s...  79.8 us
    ppermute x4, waiting for transfers between devices, cotangent_quarter(): arrived = lax.ppermute(piece, ('tok', 'tile'), pairs)  32.4 us
    dot_general x3, matrix products, dot_bf(): jnp.dot(left_part, right_part, preferred_element_type=jnp.float32)  20.1 us
    all_gather x1, waiting for transfers between devices, owner_plan(): acts = lax.all_gather(acts, 'tok', axis=0, tiled=True)  19.8 us
    dynamic_update_slice x8, local copies, waits for them, and re-layouts, owner_plan(): lax.dynamic_update_slice(cots, piece[:, None, None], (0, side, which, 0, 0))  14.4 us
    ppermute x11, starting transfers between devices, swapped(): lax.ppermute(shard, axis, [(i, i ^ 1 << stride) for i in range(lax.axis_s...  12 us
    ppermute x9, starting transfers between devices, exchange(): arrived = lax.ppermute(piece, axis, [(i, i ^ step) for i in range(size)])  11.2 us
  transfers between devices with their start and end apart: 25, of which 17 were waited for; matrix products, arithmetic and copies ran while one was open for 17% of the time, Pallas kernels for 0%

profile of v2, /device:TPU:8, one launch (start us, length us, event | category | flops | bytes accessed | tf_op | source)
XLA Modules:
  0.0 405.1 jit_solution(12563866627702051010)
XLA Ops:
  8.5 1.9 collective-permute-start.1
  10.5 4.0 collective-permute-start.2
  15.7 1.6 collective-permute-start
  20.1 5.7 %collective-permute-done.2 = bf16[1,128,1024]{2,1,0:T(8,128)(2,1)} collective-permute-done((bf16[1,128,1024]{2,1,0:T(8,128)(2,1)S(1)}, bf16[1,128,1024]{2,1,0:T(8,128)(2,1)}, u32[]{:S(2)}, u32[]{:S(2)}) %collective-permute-start.2) | collective-permute-done | bytes 262176 | tf_op jit(solution)/shard_map/ppermute | solution.py:129
  26.7 26.7 %collective-permute-done.3 = bf16[1,128,1024]{2,1,0:T(8,128)(2,1)} collective-permute-done((bf16[1,128,1024]{2,1,0:T(8,128)(2,1)S(1)}, bf16[1,128,1024]{2,1,0:T(8,128)(2,1)}, u32[]{:S(2)}, u32[]{:S(2)}) %collective-permute-start.3) | collective-permute-done | bytes 262176 | tf_op jit(solution)/shard_map/ppermute | solution.py:129
  56.5 4.2 %collective-permute-start.8 = (bf16[4,128,1024]{2,1,0:T(8,128)(2,1)S(1)}, bf16[4,128,1024]{2,1,0:T(8,128)(2,1)}, u32[]{:S(2)}, u32[]{:S(2)}) collective-permute-start(bf16[4,128,1024]{2,1,0:T(8,128)(2,1)S(1)} %constant_dynamic-update-slice_fusion.9), channel_id=1, source_target_pairs={{0,4},{2,6},{4,0},{6,2},{1,5},{3,7},{5,1},{7,3},{8,12},{10,14},{12... | collective-permute-start | bytes 3145736 | tf_op jit(solution)/shard_map/ppermute | solution.py:10
  60.7 1.5 collective-permute-start.11
  62.4 4.0 bitcast_convert_fusion
  67.1 16.8 %collective-permute-done.8 = bf16[4,128,1024]{2,1,0:T(8,128)(2,1)} collective-permute-done((bf16[4,128,1024]{2,1,0:T(8,128)(2,1)S(1)}, bf16[4,128,1024]{2,1,0:T(8,128)(2,1)}, u32[]{:S(2)}, u32[]{:S(2)}) %collective-permute-start.8) | collective-permute-done | bytes 1048608 | tf_op jit(solution)/shard_map/ppermute | solution.py:10
  86.5 1.8 pad_maximum_fusion
  88.3 4.3 %broadcast_in_dim.60 = bf16[4,2,4,128,1024]{4,3,2,1,0:T(8,128)(2,1)} broadcast(bf16[]{:T(256)} %constant.124.clone.1), dimensions={} | broadcast | bytes 8388610 | tf_op jit(solution)/shard_map/broadcast_in_dim | solution.py:157
  93.9 2.3 bitcast_dynamic-update-slice_fusion.5
  96.2 2.2 bitcast_dynamic-update-slice_fusion.4
  98.4 12.7 %collective-permute-done.12 = bf16[4,128,1024]{2,1,0:T(8,128)(2,1)} collective-permute-done((bf16[4,128,1024]{2,1,0:T(8,128)(2,1)}, bf16[4,128,1024]{2,1,0:T(8,128)(2,1)}, u32[]{:S(2)}, u32[]{:S(2)}) %collective-permute-start.12) | collective-permute-done | bytes 1048608 | tf_op jit(solution)/shard_map/ppermute | solution.py:10
  111.2 2.3 bitcast_dynamic-update-slice_fusion.3
  113.4 2.3 bitcast_dynamic-update-slice_fusion.2
  115.7 2.3 bitcast_dynamic-update-slice_fusion.1
  120.1 19.8 %all-gather.2.cloned.1.call-done = bf16[4096,512]{1,0:T(8,128)(2,1)} async-done(((bf16[1024,512]{1,0:T(8,128)(2,1)}), bf16[4096,512]{1,0:T(8,128)(2,1)}) %all-gather.2.cloned.1.call-update) | async-done | bytes 4194320 | tf_op jit(solution)/shard_map/all_gather | solution.py:156
  139.9 9.2 %convolution_convert_fusion = bf16[512,1024]{1,0:T(8,128)(2,1)S(1)} fusion(bf16[4096,512]{1,0:T(8,128)(2,1)} %all-gather.2.cloned.1.call-done, bf16[4096,1024]{1,0:T(8,128)(2,1)} %bitcast.18), kind=kOutput, calls=%fused_computation.38 | convolution fusion | flops 4295491584 | bytes 13631488 | tf_op jit(solution)/shard_map/dot_general | solution.py:176
  149.1 1.7 collective-permute-start.15
  151.6 3.0 collective-permute-start.5
  154.7 12.6 %collective-permute-done.5 = bf16[1,272,1024]{2,1,0:T(8,128)(2,1)} collective-permute-done((bf16[1,272,1024]{2,1,0:T(8,128)(2,1)}, bf16[1,272,1024]{2,1,0:T(8,128)(2,1)}, u32[]{:S(2)}, u32[]{:S(2)}) %collective-permute-start.5) | collective-permute-done | bytes 557088 | tf_op jit(solution)/shard_map/ppermute | solution.py:112
  167.3 2.2 constant_dynamic-slice_fusion.7
  170.8 1.9 collective-permute-start.7
  172.7 1.5 collective-permute-done.15
  174.3 1.7 broadcast_select_fusion.2
  176.9 1.6 pad_maximum_fusion.1
  178.5 3.9 copy.13
  182.4 24.2 %collective-permute-done.6 = bf16[1,272,1024]{2,1,0:T(8,128)(2,1)} collective-permute-done((bf16[1,272,1024]{2,1,0:T(8,128)(2,1)}, bf16[1,272,1024]{2,1,0:T(8,128)(2,1)}, u32[]{:S(2)}, u32[]{:S(2)}) %collective-permute-start.6) | collective-permute-done | bytes 557088 | tf_op jit(solution)/shard_map/ppermute | solution.py:112
  207.8 12.2 %collective-permute-done.7 = bf16[1,272,1024]{2,1,0:T(8,128)(2,1)} collective-permute-done((bf16[1,272,1024]{2,1,0:T(8,128)(2,1)}, bf16[1,272,1024]{2,1,0:T(8,128)(2,1)}, u32[]{:S(2)}, u32[]{:S(2)}) %collective-permute-start.7) | collective-permute-done | bytes 557088 | tf_op jit(solution)/shard_map/ppermute | solution.py:112
  221.3 4.7 %abs_reduce_fusion = (f32[1024]{0:T(1024)S(1)}, f32[1024,1024]{1,0:T(8,128)}) fusion(f32[1024]{0:T(1024)S(1)} %fusion.35, bf16[4,256,1024]{2,1,0:T(8,128)(2,1)S(1)} %slice.12, bf16[1024,1024]{0,1:T(8,128)(2,1)S(1)} %copy-done.7, pred[]{:T(512)S(6)} %eq.39, bf16[512,1024]{1,0:T(8,128)(2,1)S(1)} %copy-done.3, bf16[512,1024]{1,0:T(8,128)(2,1)S(1)} %get-tuple-element.22), kind=kOutput, calls=%fused_computation.15 | convolution fusion | flops 2162162688 | bytes 10493953 | tf_op jit(solution)/shard_map/dot_general | solution.py:185
  228.0 6.0 %fusion.45 = (bf16[1024,1024]{1,0:T(8,128)(2,1)S(1)}, bf16[1024,1024]{1,0:T(8,128)(2,1)}) fusion(f32[1024,1024]{1,0:T(8,128)} %get-tuple-element.34, f32[]{:T(128)S(6)} %mul_shard_map.3, f32[]{:T(128)S(6)} %mul.81, f32[1024]{0:T(1024)S(1)} %fusion.35, bf16[4,256,1024]{2,1,0:T(8,128)(2,1)} %copy-done.4), kind=kLoop, calls=%fused_computation.94 | loop fusion | flops 12582912 | bytes 10489864 | tf_op jit(solution)/shard_map/convert_element_type | solution.py:188
  234.8 11.7 %fusion.14 = bf16[1024,1024]{1,0:T(8,128)(2,1)} fusion(bf16[1024,1024]{1,0:T(8,128)(2,1)} %get-tuple-element.15), kind=kOutput, calls=%fused_computation.28 | convolution fusion | flops 4302307328 | bytes 4194304 | tf_op jit(solution)/shard_map/dot_general | solution.py:103
  246.5 4.7 %fusion.21 = bf16[1024,1024]{1,0:T(8,128)(2,1)S(1)} fusion(bf16[1024,1024]{1,0:T(8,128)(2,1)} %get-tuple-element.15, bf16[1024,1024]{1,0:T(8,128)(2,1)} %fusion.14), kind=kOutput, calls=%fused_computation.36 | convolution fusion | flops 2148532224 | bytes 6291456 | tf_op jit(solution)/shard_map/dot_general | solution.py:103
  252.4 1.9 collective-permute-start.17
  254.3 1.6 collective-permute-start.18
  255.9 3.7 fusion.24
  259.6 28.2 %collective-permute-done.17 = bf16[1,256,1024]{2,1,0:T(8,128)(2,1)S(1)} collective-permute-done((bf16[1,256,1024]{2,1,0:T(8,128)(2,1)S(1)}, bf16[1,256,1024]{2,1,0:T(8,128)(2,1)S(1)}, u32[]{:S(2)}, u32[]{:S(2)}) %collective-permute-start.17) | collective-permute-done | bytes 524320 | tf_op jit(solution)/shard_map/ppermute | solution.py:112
  287.9 12.9 %collective-permute-done.18 = bf16[1,256,1024]{2,1,0:T(8,128)(2,1)S(1)} collective-permute-done((bf16[1,256,1024]{2,1,0:T(8,128)(2,1)S(1)}, bf16[1,256,1024]{2,1,0:T(8,128)(2,1)S(1)}, u32[]{:S(2)}, u32[]{:S(2)}) %collective-permute-start.18) | collective-permute-done | bytes 524320 | tf_op jit(solution)/shard_map/ppermute | solution.py:112
  301.6 47.3 %collective-permute-done.19 = bf16[1024,1024]{1,0:T(8,128)(2,1)} collective-permute-done((bf16[1024,1024]{1,0:T(8,128)(2,1)}, bf16[1024,1024]{1,0:T(8,128)(2,1)}, u32[]{:S(2)}, u32[]{:S(2)}) %collective-permute-start.19) | collective-permute-done | bytes 2097184 | tf_op jit(solution)/shard_map/ppermute | solution.py:10
  348.8 1.8 broadcast_select_fusion
  351.7 6.5 %multiply_reduce_fusion.1 = (f32[]{:T(128)}, f32[512,1024]{1,0:T(8,128)}) fusion(bf16[1024,1024]{1,0:T(8,128)(2,1)} %collective-permute-done.19, bf16[1024,1024]{1,0:T(8,128)(2,1)} %fusion.24, pred[]{:T(512)S(6)} %eq.39, bf16[512,1024]{1,0:T(8,128)(2,1)} %bitcast.67, bf16[512,1024]{1,0:T(8,128)(2,1)} %copy-done.2, bf16[512,1024]{1,0:T(8,128)(2,1)S(1)} %get-tuple-element.22), kind=kOutput, calls=%fused_computation.23 | convolution fusion | flops 2154299392 | bytes 9437189 | tf_op jit(solution)/shard_map/dot_general | solution.py:209
  359.5 2.9 multiply_reduce_fusion
  365.0 2.0 multiply_convert_fusion
  367.1 7.5 %collective-permute-done.21 = bf16[1,128,1024]{2,1,0:T(8,128)(2,1)S(1)} collective-permute-done((bf16[1,128,1024]{2,1,0:T(8,128)(2,1)S(1)}, bf16[1,128,1024]{2,1,0:T(8,128)(2,1)S(1)}, u32[]{:S(2)}, u32[]{:S(2)}) %collective-permute-start.21) | collective-permute-done | bytes 262176 | tf_op jit(solution)/shard_map/ppermute | solution.py:112
  376.0 2.9 bitcast_add_fusion
  378.9 11.2 %collective-permute-done.22 = bf16[1,128,1024]{2,1,0:T(8,128)(2,1)S(1)} collective-permute-done((bf16[1,128,1024]{2,1,0:T(8,128)(2,1)S(1)}, bf16[1,128,1024]{2,1,0:T(8,128)(2,1)S(1)}, u32[]{:S(2)}, u32[]{:S(2)}) %collective-permute-start.22) | collective-permute-done | bytes 262176 | tf_op jit(solution)/shard_map/ppermute | solution.py:112
  390.1 7.1 %collective-permute-done.23 = bf16[1,128,1024]{2,1,0:T(8,128)(2,1)S(1)} collective-permute-done((bf16[1,128,1024]{2,1,0:T(8,128)(2,1)S(1)}, bf16[1,128,1024]{2,1,0:T(8,128)(2,1)S(1)}, u32[]{:S(2)}, u32[]{:S(2)}) %collective-permute-start.23) | collective-permute-done | bytes 262176 | tf_op jit(solution)/shard_map/ppermute | solution.py:112
  (78 shorter events, 31.3 us)
Async XLA Ops:
  7.2 132.7 %all-gather.2.cloned.1.call-start = ((), (), s32[]{:S(2)}) async-start(), calls=%async_computation | async-start | bytes 5242880 | tf_op jit(solution)/shard_map/all_gather | solution.py:156
  8.5 10.4 %collective-permute-start.1 = (bf16[1,128,1024]{2,1,0:T(8,128)(2,1)S(1)}, bf16[1,128,1024]{2,1,0:T(8,128)(2,1)}, u32[]{:S(2)}, u32[]{:S(2)}) collective-permute-start(bf16[1,128,1024]{2,1,0:T(8,128)(2,1)S(1)} %get-tuple-element.30), channel_id=1, source_target_pairs={{0,0},{2,8},{4,16},{6,24},{8,2},{10,10},{12,18},{14,26},{16,4},{18... | collective-permute-start | bytes 786440 | tf_op jit(solution)/shard_map/ppermute | solution.py:129
  10.5 15.3 %collective-permute-start.2 = (bf16[1,128,1024]{2,1,0:T(8,128)(2,1)S(1)}, bf16[1,128,1024]{2,1,0:T(8,128)(2,1)}, u32[]{:S(2)}, u32[]{:S(2)}) collective-permute-start(bf16[1,128,1024]{2,1,0:T(8,128)(2,1)S(1)} %get-tuple-element.29), channel_id=1, source_target_pairs={{0,2},{2,10},{4,18},{6,26},{8,4},{10,12},{12,20},{14,28},{16,6},{1... | collective-permute-start | bytes 786440 | tf_op jit(solution)/shard_map/ppermute | solution.py:129
  15.7 39.7 %collective-permute-start = (bf16[512,512]{1,0:T(8,128)(2,1)S(1)}, bf16[512,512]{1,0:T(8,128)(2,1)S(1)}, u32[]{:S(2)}, u32[]{:S(2)}) collective-permute-start(bf16[512,512]{1,0:T(8,128)(2,1)S(1)} %get-tuple-element.32), channel_id=1, source_target_pairs={{0,1},{1,0},{2,3},{3,2},{4,5},{5,4},{6,7},{7,6},{8,9},{9,8},{10,11... | collective-permute-start | bytes 1572872 | tf_op jit(solution)/shard_map/ppermute | solution.py:10
  17.3 36.2 %collective-permute-start.3 = (bf16[1,128,1024]{2,1,0:T(8,128)(2,1)S(1)}, bf16[1,128,1024]{2,1,0:T(8,128)(2,1)}, u32[]{:S(2)}, u32[]{:S(2)}) collective-permute-start(bf16[1,128,1024]{2,1,0:T(8,128)(2,1)S(1)} %get-tuple-element.28), channel_id=1, source_target_pairs={{0,4},{2,12},{4,20},{6,28},{8,6},{10,14},{12,22},{14,30},{16,0},{1... | collective-permute-start | bytes 786440 | tf_op jit(solution)/shard_map/ppermute | solution.py:129
  18.2 36.2 %collective-permute-start.4 = (bf16[1,128,1024]{2,1,0:T(8,128)(2,1)S(1)}, bf16[1,128,1024]{2,1,0:T(8,128)(2,1)}, u32[]{:S(2)}, u32[]{:S(2)}) collective-permute-start(bf16[1,128,1024]{2,1,0:T(8,128)(2,1)S(1)} %get-tuple-element.27), channel_id=1, source_target_pairs={{0,6},{2,14},{4,22},{6,30},{8,0},{10,8},{12,16},{14,24},{16,2},{18... | collective-permute-start | bytes 786440 | tf_op jit(solution)/shard_map/ppermute | solution.py:129
  56.5 27.4 %collective-permute-start.8 = (bf16[4,128,1024]{2,1,0:T(8,128)(2,1)S(1)}, bf16[4,128,1024]{2,1,0:T(8,128)(2,1)}, u32[]{:S(2)}, u32[]{:S(2)}) collective-permute-start(bf16[4,128,1024]{2,1,0:T(8,128)(2,1)S(1)} %constant_dynamic-update-slice_fusion.9), channel_id=1, source_target_pairs={{0,4},{2,6},{4,0},{6,2},{1,5},{3,7},{5,1},{7,3},{8,12},{10,14},{12... | collective-permute-start | bytes 3145736 | tf_op jit(solution)/shard_map/ppermute | solution.py:10
  60.7 25.6 %collective-permute-start.11 = (bf16[4,128,1024]{2,1,0:T(8,128)(2,1)S(1)}, bf16[4,128,1024]{2,1,0:T(8,128)(2,1)}, u32[]{:S(2)}, u32[]{:S(2)}) collective-permute-start(bf16[4,128,1024]{2,1,0:T(8,128)(2,1)S(1)} %constant_dynamic-update-slice_fusion.9), channel_id=1, source_target_pairs={{0,1},{1,0},{2,3},{3,2},{4,5},{5,4},{6,7},{7,6},{8,9},{9,8},{10,11... | collective-permute-start | bytes 3145736 | tf_op jit(solution)/shard_map/ppermute | solution.py:10
  62.2 4.3 %copy-start = (f32[4,1,256,1024]{3,2,1,0:T(8,128)S(1)}, f32[4,1,256,1024]{3,2,1,0:T(8,128)}, u32[]{:S(2)}) copy-start(f32[4,1,256,1024]{3,2,1,0:T(8,128)} %param.5) | copy-start | bytes 12582916
  66.4 29.8 %collective-permute-start.9 = (bf16[4,128,1024]{2,1,0:T(8,128)(2,1)S(1)}, bf16[4,128,1024]{2,1,0:T(8,128)(2,1)}, u32[]{:S(2)}, u32[]{:S(2)}) collective-permute-start(bf16[4,128,1024]{2,1,0:T(8,128)(2,1)S(1)} %constant_dynamic-update-slice_fusion.9), channel_id=1, source_target_pairs={{0,2},{2,0},{4,6},{6,4},{1,3},{3,1},{5,7},{7,5},{8,10},{10,8},{12,... | collective-permute-start | bytes 3145736 | tf_op jit(solution)/shard_map/ppermute | solution.py:10
  83.9 27.3 %collective-permute-start.10 = (bf16[4,128,1024]{2,1,0:T(8,128)(2,1)}, bf16[4,128,1024]{2,1,0:T(8,128)(2,1)}, u32[]{:S(2)}, u32[]{:S(2)}) collective-permute-start(bf16[4,128,1024]{2,1,0:T(8,128)(2,1)} %collective-permute-done.8), channel_id=1, source_target_pairs={{0,2},{2,0},{4,6},{6,4},{1,3},{3,1},{5,7},{7,5},{8,10},{10,8},{12,... | collective-permute-start | bytes 3145736 | tf_op jit(solution)/shard_map/ppermute | solution.py:10
  86.2 24.9 %collective-permute-start.12 = (bf16[4,128,1024]{2,1,0:T(8,128)(2,1)}, bf16[4,128,1024]{2,1,0:T(8,128)(2,1)}, u32[]{:S(2)}, u32[]{:S(2)}) collective-permute-start(bf16[4,128,1024]{2,1,0:T(8,128)(2,1)} %collective-permute-done.11), channel_id=1, source_target_pairs={{0,4},{2,6},{4,0},{6,2},{1,5},{3,7},{5,1},{7,3},{8,12},{10,14},{12... | collective-permute-start | bytes 3145736 | tf_op jit(solution)/shard_map/ppermute | solution.py:10
  93.6 24.4 %collective-permute-start.13 = (bf16[4,128,1024]{2,1,0:T(8,128)(2,1)}, bf16[4,128,1024]{2,1,0:T(8,128)(2,1)S(1)}, u32[]{:S(2)}, u32[]{:S(2)}) collective-permute-start(bf16[4,128,1024]{2,1,0:T(8,128)(2,1)} %collective-permute-done.11), channel_id=1, source_target_pairs={{0,2},{2,0},{4,6},{6,4},{1,3},{3,1},{5,7},{7,5},{8,10},{10,8},{12,... | collective-permute-start | bytes 3145736 | tf_op jit(solution)/shard_map/ppermute | solution.py:10
  111.2 7.8 %collective-permute-start.14 = (bf16[4,128,1024]{2,1,0:T(8,128)(2,1)}, bf16[4,128,1024]{2,1,0:T(8,128)(2,1)S(1)}, u32[]{:S(2)}, u32[]{:S(2)}) collective-permute-start(bf16[4,128,1024]{2,1,0:T(8,128)(2,1)} %collective-permute-done.12), channel_id=1, source_target_pairs={{0,2},{2,0},{4,6},{6,4},{1,3},{3,1},{5,7},{7,5},{8,10},{10,8},{12,... | collective-permute-start | bytes 3145736 | tf_op jit(solution)/shard_map/ppermute | solution.py:10
  149.1 23.7 %copy-start.8 = (bf16[512,1024]{1,0:T(8,128)(2,1)}, bf16[512,1024]{1,0:T(8,128)(2,1)S(1)}, u32[]{:S(2)}) copy-start(bf16[512,1024]{1,0:T(8,128)(2,1)S(1)} %convolution_convert_fusion) | copy-start | bytes 3145732
  149.1 25.2 %collective-permute-start.15 = (bf16[512,1024]{1,0:T(8,128)(2,1)S(1)}, bf16[512,1024]{1,0:T(8,128)(2,1)}, u32[]{:S(2)}, u32[]{:S(2)}) collective-permute-start(bf16[512,1024]{1,0:T(8,128)(2,1)S(1)} %convolution_convert_fusion), channel_id=1, source_target_pairs={{0,1},{1,0},{2,3},{3,2},{4,5},{5,4},{6,7},{7,6},{8,9},{9,8},{10,11... | collective-permute-start | bytes 3145736 | tf_op jit(solution)/shard_map/ppermute | solution.py:10
  151.6 15.7 %collective-permute-start.5 = (bf16[1,272,1024]{2,1,0:T(8,128)(2,1)}, bf16[1,272,1024]{2,1,0:T(8,128)(2,1)}, u32[]{:S(2)}, u32[]{:S(2)}) collective-permute-start(bf16[1,272,1024]{2,1,0:T(8,128)(2,1)} %constant_dynamic-slice_fusion.9), channel_id=1, source_target_pairs={{0,8},{8,0},{16,24},{24,16},{1,9},{9,1},{17,25},{25,17},{2,10},{10... | collective-permute-start | bytes 1671176 | tf_op jit(solution)/shard_map/ppermute | solution.py:112
  169.5 37.2 %collective-permute-start.6 = (bf16[1,272,1024]{2,1,0:T(8,128)(2,1)}, bf16[1,272,1024]{2,1,0:T(8,128)(2,1)}, u32[]{:S(2)}, u32[]{:S(2)}) collective-permute-start(bf16[1,272,1024]{2,1,0:T(8,128)(2,1)} %get-tuple-element.17), channel_id=1, source_target_pairs={{0,16},{8,24},{16,0},{24,8},{1,17},{9,25},{17,1},{25,9},{2,18},{10... | collective-permute-start | bytes 1671176 | tf_op jit(solution)/shard_map/ppermute | solution.py:112
  170.8 49.1 %collective-permute-start.7 = (bf16[1,272,1024]{2,1,0:T(8,128)(2,1)}, bf16[1,272,1024]{2,1,0:T(8,128)(2,1)}, u32[]{:S(2)}, u32[]{:S(2)}) collective-permute-start(bf16[1,272,1024]{2,1,0:T(8,128)(2,1)} %get-tuple-element.16), channel_id=1, source_target_pairs={{0,24},{8,16},{16,8},{24,0},{1,25},{9,17},{17,9},{25,1},{2,26},{10... | collective-permute-start | bytes 1671176 | tf_op jit(solution)/shard_map/ppermute | solution.py:112
  175.9 1.0 copy-start.2
  182.4 38.8 %copy-start.3 = (bf16[512,1024]{1,0:T(8,128)(2,1)S(1)}, bf16[512,1024]{1,0:T(8,128)(2,1)}, u32[]{:S(2)}) copy-start(bf16[512,1024]{1,0:T(8,128)(2,1)} %copy-done.2) | copy-start | bytes 3145732
  182.4 38.9 %copy-start.7 = (bf16[1024,1024]{0,1:T(8,128)(2,1)S(1)}, bf16[1024,1024]{0,1:T(8,128)(2,1)}, u32[]{:S(2)}) copy-start(bf16[1024,1024]{0,1:T(8,128)(2,1)} %copy.13) | copy-start | bytes 6291460
  221.2 4.7 %copy-start.4 = (bf16[4,256,1024]{2,1,0:T(8,128)(2,1)}, bf16[4,256,1024]{2,1,0:T(8,128)(2,1)S(1)}, u32[]{:S(2)}) copy-start(bf16[4,256,1024]{2,1,0:T(8,128)(2,1)S(1)} %slice.12) | copy-start | bytes 6291460
  234.8 16.4 %collective-permute-start.16 = (bf16[1,256,1024]{2,1,0:T(8,128)(2,1)}, bf16[1,256,1024]{2,1,0:T(8,128)(2,1)}, u32[]{:S(2)}, u32[]{:S(2)}) collective-permute-start(bf16[1,256,1024]{2,1,0:T(8,128)(2,1)} %constant_dynamic-slice_fusion.6), channel_id=1, source_target_pairs={{0,8},{8,0},{16,24},{24,16},{1,9},{9,1},{17,25},{25,17},{2,10},{10... | collective-permute-start | bytes 1572872 | tf_op jit(solution)/shard_map/ppermute | solution.py:112
  246.5 9.5 %copy-start.6 = (bf16[1024,1024]{1,0:T(8,128)(2,1)S(1)}, bf16[1024,1024]{1,0:T(8,128)(2,1)}, u32[]{:S(2)}) copy-start(bf16[1024,1024]{1,0:T(8,128)(2,1)} %get-tuple-element.15) | copy-start | bytes 6291460
  252.4 35.5 %collective-permute-start.17 = (bf16[1,256,1024]{2,1,0:T(8,128)(2,1)S(1)}, bf16[1,256,1024]{2,1,0:T(8,128)(2,1)S(1)}, u32[]{:S(2)}, u32[]{:S(2)}) collective-permute-start(bf16[1,256,1024]{2,1,0:T(8,128)(2,1)S(1)} %get-tuple-element.20), channel_id=1, source_target_pairs={{0,16},{8,24},{16,0},{24,8},{1,17},{9,25},{17,1},{25,9},{2,18},{10... | collective-permute-start | bytes 1572872 | tf_op jit(solution)/shard_map/ppermute | solution.py:112
  254.3 46.5 %collective-permute-start.18 = (bf16[1,256,1024]{2,1,0:T(8,128)(2,1)S(1)}, bf16[1,256,1024]{2,1,0:T(8,128)(2,1)S(1)}, u32[]{:S(2)}, u32[]{:S(2)}) collective-permute-start(bf16[1,256,1024]{2,1,0:T(8,128)(2,1)S(1)} %get-tuple-element.19), channel_id=1, source_target_pairs={{0,24},{8,16},{16,8},{24,0},{1,25},{9,17},{17,9},{25,1},{2,26},{10... | collective-permute-start | bytes 1572872 | tf_op jit(solution)/shard_map/ppermute | solution.py:112
  300.9 47.9 %collective-permute-start.19 = (bf16[1024,1024]{1,0:T(8,128)(2,1)}, bf16[1024,1024]{1,0:T(8,128)(2,1)}, u32[]{:S(2)}, u32[]{:S(2)}) collective-permute-start(bf16[1024,1024]{1,0:T(8,128)(2,1)} %fusion.24), channel_id=1, source_target_pairs={{0,1},{1,0},{2,3},{3,2},{4,5},{5,4},{6,7},{7,6},{8,9},{9,8},{10,11... | collective-permute-start | bytes 6291464 | tf_op jit(solution)/shard_map/ppermute | solution.py:10
  358.8 3.7 collective-permute-start.20
  365.0 11.0 %copy-start.1 = (f32[4,1,256,1024]{3,2,1,0:T(8,128)S(1)}, f32[4,1,256,1024]{3,2,1,0:T(8,128)}, u32[]{:S(2)}) copy-start(f32[4,1,256,1024]{3,2,1,0:T(8,128)} %param.5) | copy-start | bytes 12582916
  367.0 7.6 %collective-permute-start.21 = (bf16[1,128,1024]{2,1,0:T(8,128)(2,1)S(1)}, bf16[1,128,1024]{2,1,0:T(8,128)(2,1)S(1)}, u32[]{:S(2)}, u32[]{:S(2)}) collective-permute-start(bf16[1,128,1024]{2,1,0:T(8,128)(2,1)S(1)} %constant_dynamic-slice_fusion.2), channel_id=1, source_target_pairs={{0,8},{8,0},{16,24},{24,16},{1,9},{9,1},{17,25},{25,17},{2,10},{10... | collective-permute-start | bytes 786440 | tf_op jit(solution)/shard_map/ppermute | solution.py:112
  374.7 15.4 %collective-permute-start.22 = (bf16[1,128,1024]{2,1,0:T(8,128)(2,1)S(1)}, bf16[1,128,1024]{2,1,0:T(8,128)(2,1)S(1)}, u32[]{:S(2)}, u32[]{:S(2)}) collective-permute-start(bf16[1,128,1024]{2,1,0:T(8,128)(2,1)S(1)} %get-tuple-element.25), channel_id=1, source_target_pairs={{0,16},{8,24},{16,0},{24,8},{1,17},{9,25},{17,1},{25,9},{2,18},{10... | collective-permute-start | bytes 786440 | tf_op jit(solution)/shard_map/ppermute | solution.py:112
  374.8 22.4 %collective-permute-start.23 = (bf16[1,128,1024]{2,1,0:T(8,128)(2,1)S(1)}, bf16[1,128,1024]{2,1,0:T(8,128)(2,1)S(1)}, u32[]{:S(2)}, u32[]{:S(2)}) collective-permute-start(bf16[1,128,1024]{2,1,0:T(8,128)(2,1)S(1)} %get-tuple-element.24), channel_id=1, source_target_pairs={{0,24},{8,16},{16,8},{24,0},{1,25},{9,17},{17,9},{25,1},{2,26},{10... | collective-permute-start | bytes 786440 | tf_op jit(solution)/shard_map/ppermute | solution.py:112
  397.2 1.0 copy-start.5
Sparse Core Ops, SparseCore 0:
  56.6 83.2 all-gather.1

commit v3 on v2

--- a/solution.py
+++ b/solution.py
@@ -185,6 +185,7 @@
     product = lax.dot_general(
         factor_data, factor_data, (((1,), (1,)), ((), ())), preferred_element_type=jnp.float32
     )
+    product = lax.optimization_barrier(product)
     rows = exchange(product.astype(jnp.bfloat16).reshape(blocks, state_rows, order), "tok")
     updated = 0.9 * previous + 0.1 * product
     identity = jnp.eye(order, dtype=jnp.float32)
@@ -198,8 +199,8 @@
         if iteration + 1 < ITERS:
             square = dot_bf(factor, factor)
             fourth = dot_bf(square, square)
+            fourth, rows = lax.optimization_barrier((fourth, rows))
             iterate = lax.optimization_barrier(dot_bf(fourth, iterate))
-    root, rows = lax.optimization_barrier((root, rows))
     partner = swapped(root, "pair", 0)
     left = jnp.where(first, root, partner)
     right = jnp.where(first, partner, root)

time: 406 us -> 408 us (level)
  local copies, waits for them, and re-layouts: 41.1 us -> 48.6 us
  matrix products: 40.4 us -> 35.3 us
    dynamic_update_slice x6, local copies, waits for them, and re-layouts: 2.3 us -> 7.59 us  [exchange(): result = lax.dynamic_update_slice_in_dim(result, arrived, index ^ step, 0)]
    dot_general x3, matrix products: 20.1 us -> 15.7 us  [dot_bf(): jnp.dot(left_part, right_part, preferred_element_type=jnp.float32)]
  transfers between devices with their start and end apart: 25 -> 25, of which waited for: 17 -> 18; matrix products, arithmetic and copies ran while one was open for 17% -> 15% of each run, Pallas kernels for 0% -> 0%
where the time goes in v3:
time: 408 us; the launch traced here: 407 us
  waiting for transfers between devices  248 us (61%)
  local copies, waits for them, and re-layouts  48.6 us (12%)
  matrix products  35.3 us (9%)
  starting transfers between devices  29.9 us (7%)
  other arithmetic  27.9 us (7%)
  between operations  17 us (4%)
    ppermute x9, waiting for transfers between devices, exchange(): arrived = lax.ppermute(piece, axis, [(i, i ^ step) for i in range(size)])  115 us
    ppermute x11, waiting for transfers between devices, swapped(): lax.ppermute(shard, axis, [(i, i ^ 1 << stride) for i in range(lax.axis_s...  81 us
    ppermute x4, waiting for transfers between devices, cotangent_quarter(): arrived = lax.ppermute(piece, ('tok', 'tile'), pairs)  32.4 us
    all_gather x1, waiting for transfers between devices, owner_plan(): acts = lax.all_gather(acts, 'tok', axis=0, tiled=True)  19.8 us
    dot_general x3, matrix products, dot_bf(): jnp.dot(left_part, right_part, preferred_element_type=jnp.float32)  15.7 us
    dynamic_update_slice x8, local copies, waits for them, and re-layouts, owner_plan(): lax.dynamic_update_slice(cots, piece[:, None, None], (0, side, which, 0, 0))  14.5 us
    ppermute x11, starting transfers between devices, swapped(): lax.ppermute(shard, axis, [(i, i ^ 1 << stride) for i in range(lax.axis_s...  12 us
    ppermute x9, starting transfers between devices, exchange(): arrived = lax.ppermute(piece, axis, [(i, i ^ step) for i in range(size)])  10.3 us
  transfers between devices with their start and end apart: 25, of which 18 were waited for; matrix products, arithmetic and copies ran while one was open for 15% of the time, Pallas kernels for 0%

profile of v3, /device:TPU:8, one launch (start us, length us, event | category | flops | bytes accessed | tf_op | source)
XLA Modules:
  0.0 406.7 jit_solution(12006377949257576979)
XLA Ops:
  8.5 1.9 collective-permute-start.1
  10.5 4.0 collective-permute-start.2
  20.1 5.7 %collective-permute-done.2 = bf16[1,128,1024]{2,1,0:T(8,128)(2,1)} collective-permute-done((bf16[1,128,1024]{2,1,0:T(8,128)(2,1)S(1)}, bf16[1,128,1024]{2,1,0:T(8,128)(2,1)}, u32[]{:S(2)}, u32[]{:S(2)}) %collective-permute-start.2) | collective-permute-done | bytes 262176 | tf_op jit(solution)/shard_map/ppermute | solution.py:129
  26.7 26.7 %collective-permute-done.3 = bf16[1,128,1024]{2,1,0:T(8,128)(2,1)} collective-permute-done((bf16[1,128,1024]{2,1,0:T(8,128)(2,1)S(1)}, bf16[1,128,1024]{2,1,0:T(8,128)(2,1)}, u32[]{:S(2)}, u32[]{:S(2)}) %collective-permute-start.3) | collective-permute-done | bytes 262176 | tf_op jit(solution)/shard_map/ppermute | solution.py:129
  56.5 4.2 %collective-permute-start.8 = (bf16[4,128,1024]{2,1,0:T(8,128)(2,1)S(1)}, bf16[4,128,1024]{2,1,0:T(8,128)(2,1)}, u32[]{:S(2)}, u32[]{:S(2)}) collective-permute-start(bf16[4,128,1024]{2,1,0:T(8,128)(2,1)S(1)} %constant_dynamic-update-slice_fusion.9), channel_id=1, source_target_pairs={{0,4},{2,6},{4,0},{6,2},{1,5},{3,7},{5,1},{7,3},{8,12},{10,14},{12... | collective-permute-start | bytes 3145736 | tf_op jit(solution)/shard_map/ppermute | solution.py:10
  62.4 2.7 bitcast_convert_fusion
  66.2 17.6 %collective-permute-done.8 = bf16[4,128,1024]{2,1,0:T(8,128)(2,1)} collective-permute-done((bf16[4,128,1024]{2,1,0:T(8,128)(2,1)S(1)}, bf16[4,128,1024]{2,1,0:T(8,128)(2,1)}, u32[]{:S(2)}, u32[]{:S(2)}) %collective-permute-start.8) | collective-permute-done | bytes 1048608 | tf_op jit(solution)/shard_map/ppermute | solution.py:10
  88.0 4.3 %broadcast_in_dim.60 = bf16[4,2,4,128,1024]{4,3,2,1,0:T(8,128)(2,1)} broadcast(bf16[]{:T(256)} %constant.124.clone.1), dimensions={} | broadcast | bytes 8388610 | tf_op jit(solution)/shard_map/broadcast_in_dim | solution.py:157
  93.6 2.3 bitcast_dynamic-update-slice_fusion.5
  95.9 2.3 bitcast_dynamic-update-slice_fusion.4
  98.2 13.0 %collective-permute-done.12 = bf16[4,128,1024]{2,1,0:T(8,128)(2,1)} collective-permute-done((bf16[4,128,1024]{2,1,0:T(8,128)(2,1)}, bf16[4,128,1024]{2,1,0:T(8,128)(2,1)}, u32[]{:S(2)}, u32[]{:S(2)}) %collective-permute-start.12) | collective-permute-done | bytes 1048608 | tf_op jit(solution)/shard_map/ppermute | solution.py:10
  111.2 2.3 bitcast_dynamic-update-slice_fusion.3
  113.5 2.2 bitcast_dynamic-update-slice_fusion.2
  115.7 2.3 bitcast_dynamic-update-slice_fusion.1
  120.1 19.8 %all-gather.2.cloned.1.call-done = bf16[4096,512]{1,0:T(8,128)(2,1)} async-done(((bf16[1024,512]{1,0:T(8,128)(2,1)}), bf16[4096,512]{1,0:T(8,128)(2,1)}) %all-gather.2.cloned.1.call-update) | async-done | bytes 4194320 | tf_op jit(solution)/shard_map/all_gather | solution.py:156
  139.9 9.2 %convolution_convert_fusion.1 = bf16[512,1024]{1,0:T(8,128)(2,1)S(1)} fusion(bf16[4096,512]{1,0:T(8,128)(2,1)} %all-gather.2.cloned.1.call-done, bf16[4096,1024]{1,0:T(8,128)(2,1)} %bitcast.18), kind=kOutput, calls=%fused_computation.37 | convolution fusion | flops 4295491584 | bytes 13631488 | tf_op jit(solution)/shard_map/dot_general | solution.py:176
  149.1 1.7 collective-permute-start.15
  151.9 3.1 collective-permute-start.5
  155.0 12.3 %collective-permute-done.5 = bf16[1,272,1024]{2,1,0:T(8,128)(2,1)S(1)} collective-permute-done((bf16[1,272,1024]{2,1,0:T(8,128)(2,1)S(1)}, bf16[1,272,1024]{2,1,0:T(8,128)(2,1)S(1)}, u32[]{:S(2)}, u32[]{:S(2)}) %collective-permute-start.5) | collective-permute-done | bytes 557088 | tf_op jit(solution)/shard_map/ppermute | solution.py:112
  167.3 2.5 constant_dynamic-slice_fusion.7
  171.0 1.9 collective-permute-start.7
  177.3 3.9 copy.13
  181.2 4.6 %fusion.9 = f32[1024,1024]{1,0:T(8,128)S(1)} fusion(bf16[1024,1024]{0,1:T(8,128)(2,1)} %copy.13, pred[]{:T(512)S(6)} %eq.39, bf16[512,1024]{1,0:T(8,128)(2,1)S(1)} %get-tuple-element.23, bf16[512,1024]{1,0:T(8,128)(2,1)S(1)} %get-tuple-element.22), kind=kOutput, calls=%fused_computation.21 | convolution fusion | flops 2152726528 | bytes 8388609 | tf_op jit(solution)/shard_map/dot_general | solution.py:185
  185.8 21.2 %collective-permute-done.6 = bf16[1,272,1024]{2,1,0:T(8,128)(2,1)} collective-permute-done((bf16[1,272,1024]{2,1,0:T(8,128)(2,1)}, bf16[1,272,1024]{2,1,0:T(8,128)(2,1)}, u32[]{:S(2)}, u32[]{:S(2)}) %collective-permute-start.6) | collective-permute-done | bytes 557088 | tf_op jit(solution)/shard_map/ppermute | solution.py:112
  207.0 1.9 constant_dynamic-update-slice_fusion.7
  209.0 11.3 %collective-permute-done.7 = bf16[1,272,1024]{2,1,0:T(8,128)(2,1)} collective-permute-done((bf16[1,272,1024]{2,1,0:T(8,128)(2,1)}, bf16[1,272,1024]{2,1,0:T(8,128)(2,1)}, u32[]{:S(2)}, u32[]{:S(2)}) %collective-permute-start.7) | collective-permute-done | bytes 557088 | tf_op jit(solution)/shard_map/ppermute | solution.py:112
  220.3 1.9 constant_dynamic-update-slice_fusion.6
  222.2 1.8 slice.12
  227.7 5.8 %fusion.43 = (bf16[1024,1024]{1,0:T(8,128)(2,1)}, bf16[1024,1024]{1,0:T(8,128)(2,1)}) fusion(f32[1024,1024]{1,0:T(8,128)} %copy-done.2, f32[]{:T(128)S(6)} %mul_shard_map.3, f32[]{:T(128)S(6)} %mul.81, f32[1024]{0:T(1024)S(1)} %fusion.33, bf16[4,256,1024]{2,1,0:T(8,128)(2,1)S(1)} %slice.12), kind=kLoop, calls=%fused_computation.93 | loop fusion | flops 12582912 | bytes 10489864 | tf_op jit(solution)/shard_map/convert_element_type | solution.py:189
  234.8 13.7 %collective-permute-done.16 = bf16[1,256,1024]{2,1,0:T(8,128)(2,1)S(1)} collective-permute-done((bf16[1,256,1024]{2,1,0:T(8,128)(2,1)S(1)}, bf16[1,256,1024]{2,1,0:T(8,128)(2,1)S(1)}, u32[]{:S(2)}, u32[]{:S(2)}) %collective-permute-start.16) | collective-permute-done | bytes 524320 | tf_op jit(solution)/shard_map/ppermute | solution.py:112
  248.6 2.4 constant_dynamic-slice_fusion.4
  250.9 1.8 collective-permute-start.18
  252.7 8.0 %fusion.19 = bf16[1024,1024]{1,0:T(8,128)(2,1)} fusion(bf16[1024,1024]{1,0:T(8,128)(2,1)S(1)} %copy-done.6), kind=kOutput, calls=%fused_computation.34 | convolution fusion | flops 4303355904 | bytes 4194304 | tf_op jit(solution)/shard_map/dot_general | solution.py:103
  260.8 23.8 %collective-permute-done.17 = bf16[1,256,1024]{2,1,0:T(8,128)(2,1)} collective-permute-done((bf16[1,256,1024]{2,1,0:T(8,128)(2,1)}, bf16[1,256,1024]{2,1,0:T(8,128)(2,1)}, u32[]{:S(2)}, u32[]{:S(2)}) %collective-permute-start.17) | collective-permute-done | bytes 524320 | tf_op jit(solution)/shard_map/ppermute | solution.py:112
  284.6 1.9 constant_dynamic-update-slice_fusion.4
  286.4 11.5 %collective-permute-done.18 = bf16[1,256,1024]{2,1,0:T(8,128)(2,1)} collective-permute-done((bf16[1,256,1024]{2,1,0:T(8,128)(2,1)}, bf16[1,256,1024]{2,1,0:T(8,128)(2,1)}, u32[]{:S(2)}, u32[]{:S(2)}) %collective-permute-start.18) | collective-permute-done | bytes 524320 | tf_op jit(solution)/shard_map/ppermute | solution.py:112
  297.9 1.9 constant_dynamic-update-slice_fusion.3
  299.8 3.9 convolution_convert_fusion
  303.7 3.7 fusion.22
  308.0 46.4 %collective-permute-done.19 = bf16[1024,1024]{1,0:T(8,128)(2,1)} collective-permute-done((bf16[1024,1024]{1,0:T(8,128)(2,1)}, bf16[1024,1024]{1,0:T(8,128)(2,1)}, u32[]{:S(2)}, u32[]{:S(2)}) %collective-permute-start.19) | collective-permute-done | bytes 2097184 | tf_op jit(solution)/shard_map/ppermute | solution.py:10
  354.4 1.8 broadcast_select_fusion
  356.3 5.9 %multiply_reduce_fusion.1 = (f32[]{:T(128)}, f32[512,1024]{1,0:T(8,128)}) fusion(bf16[1024,1024]{1,0:T(8,128)(2,1)} %collective-permute-done.19, bf16[1024,1024]{1,0:T(8,128)(2,1)} %fusion.22, pred[]{:T(512)S(6)} %eq.39, bf16[512,1024]{1,0:T(8,128)(2,1)S(1)} %bitcast.63, bf16[512,1024]{1,0:T(8,128)(2,1)S(1)} %copy-done.4, ...), kind=kOutput, calls=%fused_computation.23 | convolution fusion | flops 2154299392 | bytes 9437189 | tf_op jit(solution)/shard_map/dot_general | solution.py:210
  363.5 1.7 multiply_reduce_fusion
  369.0 2.0 multiply_convert_fusion
  371.1 6.4 %collective-permute-done.21 = bf16[1,128,1024]{2,1,0:T(8,128)(2,1)S(1)} collective-permute-done((bf16[1,128,1024]{2,1,0:T(8,128)(2,1)S(1)}, bf16[1,128,1024]{2,1,0:T(8,128)(2,1)S(1)}, u32[]{:S(2)}, u32[]{:S(2)}) %collective-permute-start.21) | collective-permute-done | bytes 262176 | tf_op jit(solution)/shard_map/ppermute | solution.py:112
  379.7 4.5 %bitcast_add_fusion = f32[4,1,256,1024]{3,2,1,0:T(8,128)} fusion(bf16[4,256,1024]{2,1,0:T(8,128)(2,1)} %constant_dynamic-update-slice_fusion.3, f32[4,1,256,1024]{3,2,1,0:T(8,128)S(1)} %copy-done.1), kind=kLoop, calls=%fused_computation.9 | loop fusion | flops 4194304 | bytes 10485760 | tf_op jit(solution)/shard_map/add | solution.py:214
  384.1 9.4 %collective-permute-done.22 = bf16[1,128,1024]{2,1,0:T(8,128)(2,1)S(1)} collective-permute-done((bf16[1,128,1024]{2,1,0:T(8,128)(2,1)S(1)}, bf16[1,128,1024]{2,1,0:T(8,128)(2,1)S(1)}, u32[]{:S(2)}, u32[]{:S(2)}) %collective-permute-start.22) | collective-permute-done | bytes 262176 | tf_op jit(solution)/shard_map/ppermute | solution.py:112
  393.5 5.3 %collective-permute-done.23 = bf16[1,128,1024]{2,1,0:T(8,128)(2,1)S(1)} collective-permute-done((bf16[1,128,1024]{2,1,0:T(8,128)(2,1)S(1)}, bf16[1,128,1024]{2,1,0:T(8,128)(2,1)S(1)}, u32[]{:S(2)}, u32[]{:S(2)}) %collective-permute-start.23) | collective-permute-done | bytes 262176 | tf_op jit(solution)/shard_map/ppermute | solution.py:112
  (75 shorter events, 39.6 us)
Async XLA Ops:
  7.2 132.7 %all-gather.2.cloned.1.call-start = ((), (), s32[]{:S(2)}) async-start(), calls=%async_computation | async-start | bytes 5242880 | tf_op jit(solution)/shard_map/all_gather | solution.py:156
  8.5 10.4 %collective-permute-start.1 = (bf16[1,128,1024]{2,1,0:T(8,128)(2,1)S(1)}, bf16[1,128,1024]{2,1,0:T(8,128)(2,1)}, u32[]{:S(2)}, u32[]{:S(2)}) collective-permute-start(bf16[1,128,1024]{2,1,0:T(8,128)(2,1)S(1)} %get-tuple-element.30), channel_id=1, source_target_pairs={{0,0},{2,8},{4,16},{6,24},{8,2},{10,10},{12,18},{14,26},{16,4},{18... | collective-permute-start | bytes 786440 | tf_op jit(solution)/shard_map/ppermute | solution.py:129
  10.5 15.3 %collective-permute-start.2 = (bf16[1,128,1024]{2,1,0:T(8,128)(2,1)S(1)}, bf16[1,128,1024]{2,1,0:T(8,128)(2,1)}, u32[]{:S(2)}, u32[]{:S(2)}) collective-permute-start(bf16[1,128,1024]{2,1,0:T(8,128)(2,1)S(1)} %get-tuple-element.29), channel_id=1, source_target_pairs={{0,2},{2,10},{4,18},{6,26},{8,4},{10,12},{12,20},{14,28},{16,6},{1... | collective-permute-start | bytes 786440 | tf_op jit(solution)/shard_map/ppermute | solution.py:129
  15.7 39.7 %collective-permute-start = (bf16[512,512]{1,0:T(8,128)(2,1)S(1)}, bf16[512,512]{1,0:T(8,128)(2,1)S(1)}, u32[]{:S(2)}, u32[]{:S(2)}) collective-permute-start(bf16[512,512]{1,0:T(8,128)(2,1)S(1)} %get-tuple-element.32), channel_id=1, source_target_pairs={{0,1},{1,0},{2,3},{3,2},{4,5},{5,4},{6,7},{7,6},{8,9},{9,8},{10,11... | collective-permute-start | bytes 1572872 | tf_op jit(solution)/shard_map/ppermute | solution.py:10
  17.3 36.2 %collective-permute-start.3 = (bf16[1,128,1024]{2,1,0:T(8,128)(2,1)S(1)}, bf16[1,128,1024]{2,1,0:T(8,128)(2,1)}, u32[]{:S(2)}, u32[]{:S(2)}) collective-permute-start(bf16[1,128,1024]{2,1,0:T(8,128)(2,1)S(1)} %get-tuple-element.28), channel_id=1, source_target_pairs={{0,4},{2,12},{4,20},{6,28},{8,6},{10,14},{12,22},{14,30},{16,0},{1... | collective-permute-start | bytes 786440 | tf_op jit(solution)/shard_map/ppermute | solution.py:129
  18.2 36.2 %collective-permute-start.4 = (bf16[1,128,1024]{2,1,0:T(8,128)(2,1)S(1)}, bf16[1,128,1024]{2,1,0:T(8,128)(2,1)}, u32[]{:S(2)}, u32[]{:S(2)}) collective-permute-start(bf16[1,128,1024]{2,1,0:T(8,128)(2,1)S(1)} %get-tuple-element.27), channel_id=1, source_target_pairs={{0,6},{2,14},{4,22},{6,30},{8,0},{10,8},{12,16},{14,24},{16,2},{18... | collective-permute-start | bytes 786440 | tf_op jit(solution)/shard_map/ppermute | solution.py:129
  56.5 27.4 %collective-permute-start.8 = (bf16[4,128,1024]{2,1,0:T(8,128)(2,1)S(1)}, bf16[4,128,1024]{2,1,0:T(8,128)(2,1)}, u32[]{:S(2)}, u32[]{:S(2)}) collective-permute-start(bf16[4,128,1024]{2,1,0:T(8,128)(2,1)S(1)} %constant_dynamic-update-slice_fusion.9), channel_id=1, source_target_pairs={{0,4},{2,6},{4,0},{6,2},{1,5},{3,7},{5,1},{7,3},{8,12},{10,14},{12... | collective-permute-start | bytes 3145736 | tf_op jit(solution)/shard_map/ppermute | solution.py:10
  60.7 25.6 %collective-permute-start.11 = (bf16[4,128,1024]{2,1,0:T(8,128)(2,1)S(1)}, bf16[4,128,1024]{2,1,0:T(8,128)(2,1)}, u32[]{:S(2)}, u32[]{:S(2)}) collective-permute-start(bf16[4,128,1024]{2,1,0:T(8,128)(2,1)S(1)} %constant_dynamic-update-slice_fusion.9), channel_id=1, source_target_pairs={{0,1},{1,0},{2,3},{3,2},{4,5},{5,4},{6,7},{7,6},{8,9},{9,8},{10,11... | collective-permute-start | bytes 3145736 | tf_op jit(solution)/shard_map/ppermute | solution.py:10
  62.2 3.4 copy-start
  65.1 30.8 %collective-permute-start.9 = (bf16[4,128,1024]{2,1,0:T(8,128)(2,1)S(1)}, bf16[4,128,1024]{2,1,0:T(8,128)(2,1)}, u32[]{:S(2)}, u32[]{:S(2)}) collective-permute-start(bf16[4,128,1024]{2,1,0:T(8,128)(2,1)S(1)} %constant_dynamic-update-slice_fusion.9), channel_id=1, source_target_pairs={{0,2},{2,0},{4,6},{6,4},{1,3},{3,1},{5,7},{7,5},{8,10},{10,8},{12,... | collective-permute-start | bytes 3145736 | tf_op jit(solution)/shard_map/ppermute | solution.py:10
  83.9 27.3 %collective-permute-start.10 = (bf16[4,128,1024]{2,1,0:T(8,128)(2,1)}, bf16[4,128,1024]{2,1,0:T(8,128)(2,1)}, u32[]{:S(2)}, u32[]{:S(2)}) collective-permute-start(bf16[4,128,1024]{2,1,0:T(8,128)(2,1)} %collective-permute-done.8), channel_id=1, source_target_pairs={{0,2},{2,0},{4,6},{6,4},{1,3},{3,1},{5,7},{7,5},{8,10},{10,8},{12,... | collective-permute-start | bytes 3145736 | tf_op jit(solution)/shard_map/ppermute | solution.py:10
  86.2 24.9 %collective-permute-start.12 = (bf16[4,128,1024]{2,1,0:T(8,128)(2,1)}, bf16[4,128,1024]{2,1,0:T(8,128)(2,1)}, u32[]{:S(2)}, u32[]{:S(2)}) collective-permute-start(bf16[4,128,1024]{2,1,0:T(8,128)(2,1)} %collective-permute-done.11), channel_id=1, source_target_pairs={{0,4},{2,6},{4,0},{6,2},{1,5},{3,7},{5,1},{7,3},{8,12},{10,14},{12... | collective-permute-start | bytes 3145736 | tf_op jit(solution)/shard_map/ppermute | solution.py:10
  93.3 24.7 %collective-permute-start.13 = (bf16[4,128,1024]{2,1,0:T(8,128)(2,1)}, bf16[4,128,1024]{2,1,0:T(8,128)(2,1)S(1)}, u32[]{:S(2)}, u32[]{:S(2)}) collective-permute-start(bf16[4,128,1024]{2,1,0:T(8,128)(2,1)} %collective-permute-done.11), channel_id=1, source_target_pairs={{0,2},{2,0},{4,6},{6,4},{1,3},{3,1},{5,7},{7,5},{8,10},{10,8},{12,... | collective-permute-start | bytes 3145736 | tf_op jit(solution)/shard_map/ppermute | solution.py:10
  111.2 7.8 %collective-permute-start.14 = (bf16[4,128,1024]{2,1,0:T(8,128)(2,1)}, bf16[4,128,1024]{2,1,0:T(8,128)(2,1)S(1)}, u32[]{:S(2)}, u32[]{:S(2)}) collective-permute-start(bf16[4,128,1024]{2,1,0:T(8,128)(2,1)} %collective-permute-done.12), channel_id=1, source_target_pairs={{0,2},{2,0},{4,6},{6,4},{1,3},{3,1},{5,7},{7,5},{8,10},{10,8},{12,... | collective-permute-start | bytes 3145736 | tf_op jit(solution)/shard_map/ppermute | solution.py:10
  149.1 25.2 %collective-permute-start.15 = (bf16[512,1024]{1,0:T(8,128)(2,1)S(1)}, bf16[512,1024]{1,0:T(8,128)(2,1)}, u32[]{:S(2)}, u32[]{:S(2)}) collective-permute-start(bf16[512,1024]{1,0:T(8,128)(2,1)S(1)} %convolution_convert_fusion.1), channel_id=1, source_target_pairs={{0,1},{1,0},{2,3},{3,2},{4,5},{5,4},{6,7},{7,6},{8,9},{9,8},{10,11... | collective-permute-start | bytes 3145736 | tf_op jit(solution)/shard_map/ppermute | solution.py:10
  151.9 15.4 %collective-permute-start.5 = (bf16[1,272,1024]{2,1,0:T(8,128)(2,1)S(1)}, bf16[1,272,1024]{2,1,0:T(8,128)(2,1)S(1)}, u32[]{:S(2)}, u32[]{:S(2)}) collective-permute-start(bf16[1,272,1024]{2,1,0:T(8,128)(2,1)S(1)} %constant_dynamic-slice_fusion.9), channel_id=1, source_target_pairs={{0,8},{8,0},{16,24},{24,16},{1,9},{9,1},{17,25},{25,17},{2,10},{10... | collective-permute-start | bytes 1671176 | tf_op jit(solution)/shard_map/ppermute | solution.py:112
  169.8 37.2 %collective-permute-start.6 = (bf16[1,272,1024]{2,1,0:T(8,128)(2,1)}, bf16[1,272,1024]{2,1,0:T(8,128)(2,1)}, u32[]{:S(2)}, u32[]{:S(2)}) collective-permute-start(bf16[1,272,1024]{2,1,0:T(8,128)(2,1)} %get-tuple-element.17), channel_id=1, source_target_pairs={{0,16},{8,24},{16,0},{24,8},{1,17},{9,25},{17,1},{25,9},{2,18},{10... | collective-permute-start | bytes 1671176 | tf_op jit(solution)/shard_map/ppermute | solution.py:112
  171.0 49.2 %collective-permute-start.7 = (bf16[1,272,1024]{2,1,0:T(8,128)(2,1)}, bf16[1,272,1024]{2,1,0:T(8,128)(2,1)}, u32[]{:S(2)}, u32[]{:S(2)}) collective-permute-start(bf16[1,272,1024]{2,1,0:T(8,128)(2,1)} %get-tuple-element.16), channel_id=1, source_target_pairs={{0,24},{8,16},{16,8},{24,0},{1,25},{9,17},{17,9},{25,1},{2,26},{10... | collective-permute-start | bytes 1671176 | tf_op jit(solution)/shard_map/ppermute | solution.py:112
  175.6 5.6 %copy-start.3 = (bf16[512,1024]{1,0:T(8,128)(2,1)}, bf16[512,1024]{1,0:T(8,128)(2,1)S(1)}, u32[]{:S(2)}) copy-start(bf16[512,1024]{1,0:T(8,128)(2,1)S(1)} %get-tuple-element.23) | copy-start | bytes 3145732
  185.8 39.0 %copy-start.2 = (f32[1024,1024]{1,0:T(8,128)}, f32[1024,1024]{1,0:T(8,128)S(1)}, u32[]{:S(2)}) copy-start(f32[1024,1024]{1,0:T(8,128)S(1)} %fusion.9) | copy-start | bytes 12582916
  233.5 19.2 %copy-start.6 = (bf16[1024,1024]{1,0:T(8,128)(2,1)S(1)}, bf16[1024,1024]{1,0:T(8,128)(2,1)}, u32[]{:S(2)}) copy-start(bf16[1024,1024]{1,0:T(8,128)(2,1)} %get-tuple-element.15) | copy-start | bytes 6291460
  234.8 13.8 %collective-permute-start.16 = (bf16[1,256,1024]{2,1,0:T(8,128)(2,1)S(1)}, bf16[1,256,1024]{2,1,0:T(8,128)(2,1)S(1)}, u32[]{:S(2)}, u32[]{:S(2)}) collective-permute-start(bf16[1,256,1024]{2,1,0:T(8,128)(2,1)S(1)} %constant_dynamic-slice_fusion.6), channel_id=1, source_target_pairs={{0,8},{8,0},{16,24},{24,16},{1,9},{9,1},{17,25},{25,17},{2,10},{10... | collective-permute-start | bytes 1572872 | tf_op jit(solution)/shard_map/ppermute | solution.py:112
  250.9 33.6 %collective-permute-start.17 = (bf16[1,256,1024]{2,1,0:T(8,128)(2,1)}, bf16[1,256,1024]{2,1,0:T(8,128)(2,1)}, u32[]{:S(2)}, u32[]{:S(2)}) collective-permute-start(bf16[1,256,1024]{2,1,0:T(8,128)(2,1)} %get-tuple-element.20), channel_id=1, source_target_pairs={{0,16},{8,24},{16,0},{24,8},{1,17},{9,25},{17,1},{25,9},{2,18},{10... | collective-permute-start | bytes 1572872 | tf_op jit(solution)/shard_map/ppermute | solution.py:112
  250.9 46.9 %collective-permute-start.18 = (bf16[1,256,1024]{2,1,0:T(8,128)(2,1)}, bf16[1,256,1024]{2,1,0:T(8,128)(2,1)}, u32[]{:S(2)}, u32[]{:S(2)}) collective-permute-start(bf16[1,256,1024]{2,1,0:T(8,128)(2,1)} %get-tuple-element.19), channel_id=1, source_target_pairs={{0,24},{8,16},{16,8},{24,0},{1,25},{9,17},{17,9},{25,1},{2,26},{10... | collective-permute-start | bytes 1572872 | tf_op jit(solution)/shard_map/ppermute | solution.py:112
  307.4 47.0 %collective-permute-start.19 = (bf16[1024,1024]{1,0:T(8,128)(2,1)}, bf16[1024,1024]{1,0:T(8,128)(2,1)}, u32[]{:S(2)}, u32[]{:S(2)}) collective-permute-start(bf16[1024,1024]{1,0:T(8,128)(2,1)} %fusion.22), channel_id=1, source_target_pairs={{0,1},{1,0},{2,3},{3,2},{4,5},{5,4},{6,7},{7,6},{8,9},{9,8},{10,11... | collective-permute-start | bytes 6291464 | tf_op jit(solution)/shard_map/ppermute | solution.py:10
  308.0 48.3 %copy-start.4 = (bf16[512,1024]{1,0:T(8,128)(2,1)S(1)}, bf16[512,1024]{1,0:T(8,128)(2,1)}, u32[]{:S(2)}) copy-start(bf16[512,1024]{1,0:T(8,128)(2,1)} %copy-done.3) | copy-start | bytes 3145732
  362.8 3.7 collective-permute-start.20
  369.0 10.7 %copy-start.1 = (f32[4,1,256,1024]{3,2,1,0:T(8,128)S(1)}, f32[4,1,256,1024]{3,2,1,0:T(8,128)}, u32[]{:S(2)}) copy-start(f32[4,1,256,1024]{3,2,1,0:T(8,128)} %param.5) | copy-start | bytes 12582916
  371.1 6.4 %collective-permute-start.21 = (bf16[1,128,1024]{2,1,0:T(8,128)(2,1)S(1)}, bf16[1,128,1024]{2,1,0:T(8,128)(2,1)S(1)}, u32[]{:S(2)}, u32[]{:S(2)}) collective-permute-start(bf16[1,128,1024]{2,1,0:T(8,128)(2,1)S(1)} %constant_dynamic-slice_fusion.2), channel_id=1, source_target_pairs={{0,8},{8,0},{16,24},{24,16},{1,9},{9,1},{17,25},{25,17},{2,10},{10... | collective-permute-start | bytes 786440 | tf_op jit(solution)/shard_map/ppermute | solution.py:112
  377.6 16.0 %collective-permute-start.22 = (bf16[1,128,1024]{2,1,0:T(8,128)(2,1)S(1)}, bf16[1,128,1024]{2,1,0:T(8,128)(2,1)S(1)}, u32[]{:S(2)}, u32[]{:S(2)}) collective-permute-start(bf16[1,128,1024]{2,1,0:T(8,128)(2,1)S(1)} %get-tuple-element.25), channel_id=1, source_target_pairs={{0,16},{8,24},{16,0},{24,8},{1,17},{9,25},{17,1},{25,9},{2,18},{10... | collective-permute-start | bytes 786440 | tf_op jit(solution)/shard_map/ppermute | solution.py:112
  378.6 20.2 %collective-permute-start.23 = (bf16[1,128,1024]{2,1,0:T(8,128)(2,1)S(1)}, bf16[1,128,1024]{2,1,0:T(8,128)(2,1)S(1)}, u32[]{:S(2)}, u32[]{:S(2)}) collective-permute-start(bf16[1,128,1024]{2,1,0:T(8,128)(2,1)S(1)} %get-tuple-element.24), channel_id=1, source_target_pairs={{0,24},{8,16},{16,8},{24,0},{1,25},{9,17},{17,9},{25,1},{2,26},{10... | collective-permute-start | bytes 786440 | tf_op jit(solution)/shard_map/ppermute | solution.py:112
  398.8 1.0 copy-start.5
Sparse Core Ops, SparseCore 0:
  56.6 83.2 all-gather.1

commit v4 on v3

--- a/solution.py
+++ b/solution.py
@@ -199,9 +199,9 @@
         if iteration + 1 < ITERS:
             square = dot_bf(factor, factor)
             fourth = dot_bf(square, square)
-            fourth, rows = lax.optimization_barrier((fourth, rows))
             iterate = lax.optimization_barrier(dot_bf(fourth, iterate))
     partner = swapped(root, "pair", 0)
+    partner, rows = lax.optimization_barrier((partner, rows))
     left = jnp.where(first, root, partner)
     right = jnp.where(first, partner, root)
     left = left.reshape(blocks, 2, -1, order)

time: 408 us -> 375 us (0.919)
  waiting for transfers between devices: 248 us -> 213 us
  matrix products: 35.3 us -> 39.8 us
    ppermute x11, waiting for transfers between devices: 81 us -> 33.3 us  [swapped(): lax.ppermute(shard, axis, [(i, i ^ 1 << stride) for i in range(lax.axis_s...]
    ppermute x9, waiting for transfers between devices: 115 us -> 128 us  [exchange(): arrived = lax.ppermute(piece, axis, [(i, i ^ step) for i in range(size)])]
  transfers between devices with their start and end apart: 25 -> 25, of which waited for: 18 -> 16; matrix products, arithmetic and copies ran while one was open for 15% -> 15% of each run, Pallas kernels for 0% -> 0%
where the time goes in v4:
time: 375 us; the launch traced here: 374 us
  waiting for transfers between devices  213 us (57%)
  local copies, waits for them, and re-layouts  45.5 us (12%)
  matrix products  39.8 us (11%)
  starting transfers between devices  30.4 us (8%)
  other arithmetic  27.6 us (7%)
  between operations  17 us (5%)
    ppermute x9, waiting for transfers between devices, exchange(): arrived = lax.ppermute(piece, axis, [(i, i ^ step) for i in range(size)])  128 us
    ppermute x11, waiting for transfers between devices, swapped(): lax.ppermute(shard, axis, [(i, i ^ 1 << stride) for i in range(lax.axis_s...  33.3 us
    ppermute x4, waiting for transfers between devices, cotangent_quarter(): arrived = lax.ppermute(piece, ('tok', 'tile'), pairs)  32.4 us
    all_gather x1, waiting for transfers between devices, owner_plan(): acts = lax.all_gather(acts, 'tok', axis=0, tiled=True)  19.8 us
    dot_general x3, matrix products, dot_bf(): jnp.dot(left_part, right_part, preferred_element_type=jnp.float32)  19.5 us
    dynamic_update_slice x8, local copies, waits for them, and re-layouts, owner_plan(): lax.dynamic_update_slice(cots, piece[:, None, None], (0, side, which, 0, 0))  14.5 us
    ppermute x11, starting transfers between devices, swapped(): lax.ppermute(shard, axis, [(i, i ^ 1 << stride) for i in range(lax.axis_s...  12.8 us
    ppermute x9, starting transfers between devices, exchange(): arrived = lax.ppermute(piece, axis, [(i, i ^ step) for i in range(size)])  9.94 us
  transfers between devices with their start and end apart: 25, of which 16 were waited for; matrix products, arithmetic and copies ran while one was open for 15% of the time, Pallas kernels for 0%

profile of v4, /device:TPU:8, one launch (start us, length us, event | category | flops | bytes accessed | tf_op | source)
XLA Modules:
  0.0 373.6 jit_solution(5001949238548180859)
XLA Ops:
  8.5 1.9 collective-permute-start.1
  10.5 4.0 %collective-permute-start.2 = (bf16[1,128,1024]{2,1,0:T(8,128)(2,1)S(1)}, bf16[1,128,1024]{2,1,0:T(8,128)(2,1)}, u32[]{:S(2)}, u32[]{:S(2)}) collective-permute-start(bf16[1,128,1024]{2,1,0:T(8,128)(2,1)S(1)} %get-tuple-element.29), channel_id=1, source_target_pairs={{0,2},{2,10},{4,18},{6,26},{8,4},{10,12},{12,20},{14,28},{16,6},{1... | collective-permute-start | bytes 786440 | tf_op jit(solution)/shard_map/ppermute | solution.py:129
  15.7 1.6 collective-permute-start
  20.1 5.7 %collective-permute-done.2 = bf16[1,128,1024]{2,1,0:T(8,128)(2,1)} collective-permute-done((bf16[1,128,1024]{2,1,0:T(8,128)(2,1)S(1)}, bf16[1,128,1024]{2,1,0:T(8,128)(2,1)}, u32[]{:S(2)}, u32[]{:S(2)}) %collective-permute-start.2) | collective-permute-done | bytes 262176 | tf_op jit(solution)/shard_map/ppermute | solution.py:129
  26.7 26.7 %collective-permute-done.3 = bf16[1,128,1024]{2,1,0:T(8,128)(2,1)} collective-permute-done((bf16[1,128,1024]{2,1,0:T(8,128)(2,1)S(1)}, bf16[1,128,1024]{2,1,0:T(8,128)(2,1)}, u32[]{:S(2)}, u32[]{:S(2)}) %collective-permute-start.3) | collective-permute-done | bytes 262176 | tf_op jit(solution)/shard_map/ppermute | solution.py:129
  56.5 4.2 %collective-permute-start.8 = (bf16[4,128,1024]{2,1,0:T(8,128)(2,1)S(1)}, bf16[4,128,1024]{2,1,0:T(8,128)(2,1)}, u32[]{:S(2)}, u32[]{:S(2)}) collective-permute-start(bf16[4,128,1024]{2,1,0:T(8,128)(2,1)S(1)} %constant_dynamic-update-slice_fusion.9), channel_id=1, source_target_pairs={{0,4},{2,6},{4,0},{6,2},{1,5},{3,7},{5,1},{7,3},{8,12},{10,14},{12... | collective-permute-start | bytes 3145736 | tf_op jit(solution)/shard_map/ppermute | solution.py:10
  60.7 1.5 collective-permute-start.11
  62.4 2.7 bitcast_convert_fusion
  66.2 17.6 %collective-permute-done.8 = bf16[4,128,1024]{2,1,0:T(8,128)(2,1)} collective-permute-done((bf16[4,128,1024]{2,1,0:T(8,128)(2,1)S(1)}, bf16[4,128,1024]{2,1,0:T(8,128)(2,1)}, u32[]{:S(2)}, u32[]{:S(2)}) %collective-permute-start.8) | collective-permute-done | bytes 1048608 | tf_op jit(solution)/shard_map/ppermute | solution.py:10
  86.5 1.5 pad_maximum_fusion
  88.0 4.3 %broadcast_in_dim.60 = bf16[4,2,4,128,1024]{4,3,2,1,0:T(8,128)(2,1)} broadcast(bf16[]{:T(256)} %constant.124.clone.1), dimensions={} | broadcast | bytes 8388610 | tf_op jit(solution)/shard_map/broadcast_in_dim | solution.py:157
  93.7 2.3 bitcast_dynamic-update-slice_fusion.5
  96.0 2.3 bitcast_dynamic-update-slice_fusion.4
  98.2 13.0 %collective-permute-done.12 = bf16[4,128,1024]{2,1,0:T(8,128)(2,1)} collective-permute-done((bf16[4,128,1024]{2,1,0:T(8,128)(2,1)}, bf16[4,128,1024]{2,1,0:T(8,128)(2,1)}, u32[]{:S(2)}, u32[]{:S(2)}) %collective-permute-start.12) | collective-permute-done | bytes 1048608 | tf_op jit(solution)/shard_map/ppermute | solution.py:10
  111.2 2.3 bitcast_dynamic-update-slice_fusion.3
  113.5 2.2 bitcast_dynamic-update-slice_fusion.2
  115.7 2.3 bitcast_dynamic-update-slice_fusion.1
  120.1 19.8 %all-gather.2.cloned.1.call-done = bf16[4096,512]{1,0:T(8,128)(2,1)} async-done(((bf16[1024,512]{1,0:T(8,128)(2,1)}), bf16[4096,512]{1,0:T(8,128)(2,1)}) %all-gather.2.cloned.1.call-update) | async-done | bytes 4194320 | tf_op jit(solution)/shard_map/all_gather | solution.py:156
  139.9 9.2 %convolution_convert_fusion = bf16[512,1024]{1,0:T(8,128)(2,1)S(1)} fusion(bf16[4096,512]{1,0:T(8,128)(2,1)} %all-gather.2.cloned.1.call-done, bf16[4096,1024]{1,0:T(8,128)(2,1)} %bitcast.18), kind=kOutput, calls=%fused_computation.38 | convolution fusion | flops 4295491584 | bytes 13631488 | tf_op jit(solution)/shard_map/dot_general | solution.py:176
  149.1 1.7 collective-permute-start.15
  151.9 3.1 collective-permute-start.5
  155.0 12.3 %collective-permute-done.5 = bf16[1,272,1024]{2,1,0:T(8,128)(2,1)S(1)} collective-permute-done((bf16[1,272,1024]{2,1,0:T(8,128)(2,1)S(1)}, bf16[1,272,1024]{2,1,0:T(8,128)(2,1)S(1)}, u32[]{:S(2)}, u32[]{:S(2)}) %collective-permute-start.5) | collective-permute-done | bytes 557088 | tf_op jit(solution)/shard_map/ppermute | solution.py:112
  167.3 2.5 constant_dynamic-slice_fusion.7
  171.0 1.9 collective-permute-start.7
  175.6 1.6 pad_maximum_fusion.1
  177.2 3.9 %copy.13 = bf16[1024,1024]{0,1:T(8,128)(2,1)} copy(bf16[1024,1024]{1,0:T(8,128)(2,1)} %pad_maximum_fusion.1) | data formatting | bytes 4194304 | tf_op jit(solution)/shard_map/concatenate | solution.py:181
  181.2 4.6 %fusion.9 = f32[1024,1024]{1,0:T(8,128)S(1)} fusion(bf16[1024,1024]{0,1:T(8,128)(2,1)} %copy.13, pred[]{:T(512)S(6)} %eq.39, bf16[512,1024]{1,0:T(8,128)(2,1)S(1)} %get-tuple-element.23, bf16[512,1024]{1,0:T(8,128)(2,1)S(1)} %get-tuple-element.22), kind=kOutput, calls=%fused_computation.21 | convolution fusion | flops 2152726528 | bytes 8388609 | tf_op jit(solution)/shard_map/dot_general | solution.py:185
  185.8 21.2 %collective-permute-done.6 = bf16[1,272,1024]{2,1,0:T(8,128)(2,1)} collective-permute-done((bf16[1,272,1024]{2,1,0:T(8,128)(2,1)}, bf16[1,272,1024]{2,1,0:T(8,128)(2,1)}, u32[]{:S(2)}, u32[]{:S(2)}) %collective-permute-start.6) | collective-permute-done | bytes 557088 | tf_op jit(solution)/shard_map/ppermute | solution.py:112
  207.0 1.9 constant_dynamic-update-slice_fusion.7
  208.9 11.3 %collective-permute-done.7 = bf16[1,272,1024]{2,1,0:T(8,128)(2,1)} collective-permute-done((bf16[1,272,1024]{2,1,0:T(8,128)(2,1)}, bf16[1,272,1024]{2,1,0:T(8,128)(2,1)}, u32[]{:S(2)}, u32[]{:S(2)}) %collective-permute-start.7) | collective-permute-done | bytes 557088 | tf_op jit(solution)/shard_map/ppermute | solution.py:112
  220.3 1.9 constant_dynamic-update-slice_fusion.6
  222.2 1.8 slice.12
  227.8 5.8 %fusion.45 = (bf16[1024,1024]{1,0:T(8,128)(2,1)}, bf16[1024,1024]{1,0:T(8,128)(2,1)}) fusion(f32[1024,1024]{1,0:T(8,128)} %copy-done.2, f32[]{:T(128)S(6)} %mul_shard_map.3, f32[]{:T(128)S(6)} %mul.81, f32[1024]{0:T(1024)S(1)} %fusion.35, bf16[4,256,1024]{2,1,0:T(8,128)(2,1)S(1)} %slice.12), kind=kLoop, calls=%fused_computation.94 | loop fusion | flops 12582912 | bytes 10489864 | tf_op jit(solution)/shard_map/convert_element_type | solution.py:189
  233.6 11.7 %fusion.14 = bf16[1024,1024]{1,0:T(8,128)(2,1)} fusion(bf16[1024,1024]{1,0:T(8,128)(2,1)} %get-tuple-element.15), kind=kOutput, calls=%fused_computation.28 | convolution fusion | flops 4302307328 | bytes 4194304 | tf_op jit(solution)/shard_map/dot_general | solution.py:103
  245.3 4.1 %fusion.21 = bf16[1024,1024]{1,0:T(8,128)(2,1)S(1)} fusion(bf16[1024,1024]{1,0:T(8,128)(2,1)S(1)} %copy-done.6, bf16[1024,1024]{1,0:T(8,128)(2,1)} %fusion.14), kind=kOutput, calls=%fused_computation.36 | convolution fusion | flops 2148532224 | bytes 6291456 | tf_op jit(solution)/shard_map/dot_general | solution.py:103
  249.4 3.7 fusion.24
  253.8 13.4 %collective-permute-done.17 = bf16[1,256,1024]{2,1,0:T(8,128)(2,1)S(1)} collective-permute-done((bf16[1,256,1024]{2,1,0:T(8,128)(2,1)S(1)}, bf16[1,256,1024]{2,1,0:T(8,128)(2,1)S(1)}, u32[]{:S(2)}, u32[]{:S(2)}) %collective-permute-start.17) | collective-permute-done | bytes 524320 | tf_op jit(solution)/shard_map/ppermute | solution.py:112
  268.4 1.7 collective-permute-start.19
  270.1 31.6 %collective-permute-done.18 = bf16[1,256,1024]{2,1,0:T(8,128)(2,1)} collective-permute-done((bf16[1,256,1024]{2,1,0:T(8,128)(2,1)}, bf16[1,256,1024]{2,1,0:T(8,128)(2,1)}, u32[]{:S(2)}, u32[]{:S(2)}) %collective-permute-start.18) | collective-permute-done | bytes 524320 | tf_op jit(solution)/shard_map/ppermute | solution.py:112
  302.8 12.3 %collective-permute-done.19 = bf16[1,256,1024]{2,1,0:T(8,128)(2,1)} collective-permute-done((bf16[1,256,1024]{2,1,0:T(8,128)(2,1)}, bf16[1,256,1024]{2,1,0:T(8,128)(2,1)}, u32[]{:S(2)}, u32[]{:S(2)}) %collective-permute-start.19) | collective-permute-done | bytes 524320 | tf_op jit(solution)/shard_map/ppermute | solution.py:112
  316.2 1.8 broadcast_select_fusion
  319.1 6.6 %multiply_reduce_fusion.1 = (f32[]{:T(128)}, f32[512,1024]{1,0:T(8,128)}) fusion(bf16[1024,1024]{1,0:T(8,128)(2,1)} %collective-permute-done.16, bf16[1024,1024]{1,0:T(8,128)(2,1)} %fusion.24, pred[]{:T(512)S(6)} %eq.39, bf16[512,1024]{1,0:T(8,128)(2,1)} %bitcast.65, bf16[512,1024]{1,0:T(8,128)(2,1)} %copy-done.4, bf16[512,1024]{1,0:T(8,128)(2,1)S(1)} %get-tuple-element.22), kind=kOutput, calls=%fused_computation.23 | convolution fusion | flops 2154299392 | bytes 9437189 | tf_op jit(solution)/shard_map/dot_general | solution.py:210
  327.8 2.9 multiply_reduce_fusion
  333.3 2.0 multiply_convert_fusion
  335.4 7.0 %collective-permute-done.21 = bf16[1,128,1024]{2,1,0:T(8,128)(2,1)S(1)} collective-permute-done((bf16[1,128,1024]{2,1,0:T(8,128)(2,1)S(1)}, bf16[1,128,1024]{2,1,0:T(8,128)(2,1)S(1)}, u32[]{:S(2)}, u32[]{:S(2)}) %collective-permute-start.21) | collective-permute-done | bytes 262176 | tf_op jit(solution)/shard_map/ppermute | solution.py:112
  344.3 2.9 bitcast_add_fusion
  347.2 13.3 %collective-permute-done.22 = bf16[1,128,1024]{2,1,0:T(8,128)(2,1)S(1)} collective-permute-done((bf16[1,128,1024]{2,1,0:T(8,128)(2,1)S(1)}, bf16[1,128,1024]{2,1,0:T(8,128)(2,1)S(1)}, u32[]{:S(2)}, u32[]{:S(2)}) %collective-permute-start.22) | collective-permute-done | bytes 262176 | tf_op jit(solution)/shard_map/ppermute | solution.py:112
  360.5 5.3 %collective-permute-done.23 = bf16[1,128,1024]{2,1,0:T(8,128)(2,1)S(1)} collective-permute-done((bf16[1,128,1024]{2,1,0:T(8,128)(2,1)S(1)}, bf16[1,128,1024]{2,1,0:T(8,128)(2,1)S(1)}, u32[]{:S(2)}, u32[]{:S(2)}) %collective-permute-start.23) | collective-permute-done | bytes 262176 | tf_op jit(solution)/shard_map/ppermute | solution.py:112
  (77 shorter events, 35.7 us)
Async XLA Ops:
  7.2 132.7 %all-gather.2.cloned.1.call-start = ((), (), s32[]{:S(2)}) async-start(), calls=%async_computation | async-start | bytes 5242880 | tf_op jit(solution)/shard_map/all_gather | solution.py:156
  8.5 10.4 %collective-permute-start.1 = (bf16[1,128,1024]{2,1,0:T(8,128)(2,1)S(1)}, bf16[1,128,1024]{2,1,0:T(8,128)(2,1)}, u32[]{:S(2)}, u32[]{:S(2)}) collective-permute-start(bf16[1,128,1024]{2,1,0:T(8,128)(2,1)S(1)} %get-tuple-element.30), channel_id=1, source_target_pairs={{0,0},{2,8},{4,16},{6,24},{8,2},{10,10},{12,18},{14,26},{16,4},{18... | collective-permute-start | bytes 786440 | tf_op jit(solution)/shard_map/ppermute | solution.py:129
  10.5 15.3 %collective-permute-start.2 = (bf16[1,128,1024]{2,1,0:T(8,128)(2,1)S(1)}, bf16[1,128,1024]{2,1,0:T(8,128)(2,1)}, u32[]{:S(2)}, u32[]{:S(2)}) collective-permute-start(bf16[1,128,1024]{2,1,0:T(8,128)(2,1)S(1)} %get-tuple-element.29), channel_id=1, source_target_pairs={{0,2},{2,10},{4,18},{6,26},{8,4},{10,12},{12,20},{14,28},{16,6},{1... | collective-permute-start | bytes 786440 | tf_op jit(solution)/shard_map/ppermute | solution.py:129
  15.7 39.7 %collective-permute-start = (bf16[512,512]{1,0:T(8,128)(2,1)S(1)}, bf16[512,512]{1,0:T(8,128)(2,1)S(1)}, u32[]{:S(2)}, u32[]{:S(2)}) collective-permute-start(bf16[512,512]{1,0:T(8,128)(2,1)S(1)} %get-tuple-element.32), channel_id=1, source_target_pairs={{0,1},{1,0},{2,3},{3,2},{4,5},{5,4},{6,7},{7,6},{8,9},{9,8},{10,11... | collective-permute-start | bytes 1572872 | tf_op jit(solution)/shard_map/ppermute | solution.py:10
  17.3 36.2 %collective-permute-start.3 = (bf16[1,128,1024]{2,1,0:T(8,128)(2,1)S(1)}, bf16[1,128,1024]{2,1,0:T(8,128)(2,1)}, u32[]{:S(2)}, u32[]{:S(2)}) collective-permute-start(bf16[1,128,1024]{2,1,0:T(8,128)(2,1)S(1)} %get-tuple-element.28), channel_id=1, source_target_pairs={{0,4},{2,12},{4,20},{6,28},{8,6},{10,14},{12,22},{14,30},{16,0},{1... | collective-permute-start | bytes 786440 | tf_op jit(solution)/shard_map/ppermute | solution.py:129
  18.2 36.2 %collective-permute-start.4 = (bf16[1,128,1024]{2,1,0:T(8,128)(2,1)S(1)}, bf16[1,128,1024]{2,1,0:T(8,128)(2,1)}, u32[]{:S(2)}, u32[]{:S(2)}) collective-permute-start(bf16[1,128,1024]{2,1,0:T(8,128)(2,1)S(1)} %get-tuple-element.27), channel_id=1, source_target_pairs={{0,6},{2,14},{4,22},{6,30},{8,0},{10,8},{12,16},{14,24},{16,2},{18... | collective-permute-start | bytes 786440 | tf_op jit(solution)/shard_map/ppermute | solution.py:129
  56.5 27.4 %collective-permute-start.8 = (bf16[4,128,1024]{2,1,0:T(8,128)(2,1)S(1)}, bf16[4,128,1024]{2,1,0:T(8,128)(2,1)}, u32[]{:S(2)}, u32[]{:S(2)}) collective-permute-start(bf16[4,128,1024]{2,1,0:T(8,128)(2,1)S(1)} %constant_dynamic-update-slice_fusion.9), channel_id=1, source_target_pairs={{0,4},{2,6},{4,0},{6,2},{1,5},{3,7},{5,1},{7,3},{8,12},{10,14},{12... | collective-permute-start | bytes 3145736 | tf_op jit(solution)/shard_map/ppermute | solution.py:10
  60.7 25.6 %collective-permute-start.11 = (bf16[4,128,1024]{2,1,0:T(8,128)(2,1)S(1)}, bf16[4,128,1024]{2,1,0:T(8,128)(2,1)}, u32[]{:S(2)}, u32[]{:S(2)}) collective-permute-start(bf16[4,128,1024]{2,1,0:T(8,128)(2,1)S(1)} %constant_dynamic-update-slice_fusion.9), channel_id=1, source_target_pairs={{0,1},{1,0},{2,3},{3,2},{4,5},{5,4},{6,7},{7,6},{8,9},{9,8},{10,11... | collective-permute-start | bytes 3145736 | tf_op jit(solution)/shard_map/ppermute | solution.py:10
  62.2 3.4 copy-start
  65.1 30.9 %collective-permute-start.9 = (bf16[4,128,1024]{2,1,0:T(8,128)(2,1)S(1)}, bf16[4,128,1024]{2,1,0:T(8,128)(2,1)}, u32[]{:S(2)}, u32[]{:S(2)}) collective-permute-start(bf16[4,128,1024]{2,1,0:T(8,128)(2,1)S(1)} %constant_dynamic-update-slice_fusion.9), channel_id=1, source_target_pairs={{0,2},{2,0},{4,6},{6,4},{1,3},{3,1},{5,7},{7,5},{8,10},{10,8},{12,... | collective-permute-start | bytes 3145736 | tf_op jit(solution)/shard_map/ppermute | solution.py:10
  83.9 27.3 %collective-permute-start.10 = (bf16[4,128,1024]{2,1,0:T(8,128)(2,1)}, bf16[4,128,1024]{2,1,0:T(8,128)(2,1)}, u32[]{:S(2)}, u32[]{:S(2)}) collective-permute-start(bf16[4,128,1024]{2,1,0:T(8,128)(2,1)} %collective-permute-done.8), channel_id=1, source_target_pairs={{0,2},{2,0},{4,6},{6,4},{1,3},{3,1},{5,7},{7,5},{8,10},{10,8},{12,... | collective-permute-start | bytes 3145736 | tf_op jit(solution)/shard_map/ppermute | solution.py:10
  86.2 24.9 %collective-permute-start.12 = (bf16[4,128,1024]{2,1,0:T(8,128)(2,1)}, bf16[4,128,1024]{2,1,0:T(8,128)(2,1)}, u32[]{:S(2)}, u32[]{:S(2)}) collective-permute-start(bf16[4,128,1024]{2,1,0:T(8,128)(2,1)} %collective-permute-done.11), channel_id=1, source_target_pairs={{0,4},{2,6},{4,0},{6,2},{1,5},{3,7},{5,1},{7,3},{8,12},{10,14},{12... | collective-permute-start | bytes 3145736 | tf_op jit(solution)/shard_map/ppermute | solution.py:10
  93.4 24.6 %collective-permute-start.13 = (bf16[4,128,1024]{2,1,0:T(8,128)(2,1)}, bf16[4,128,1024]{2,1,0:T(8,128)(2,1)S(1)}, u32[]{:S(2)}, u32[]{:S(2)}) collective-permute-start(bf16[4,128,1024]{2,1,0:T(8,128)(2,1)} %collective-permute-done.11), channel_id=1, source_target_pairs={{0,2},{2,0},{4,6},{6,4},{1,3},{3,1},{5,7},{7,5},{8,10},{10,8},{12,... | collective-permute-start | bytes 3145736 | tf_op jit(solution)/shard_map/ppermute | solution.py:10
  111.2 7.8 %collective-permute-start.14 = (bf16[4,128,1024]{2,1,0:T(8,128)(2,1)}, bf16[4,128,1024]{2,1,0:T(8,128)(2,1)S(1)}, u32[]{:S(2)}, u32[]{:S(2)}) collective-permute-start(bf16[4,128,1024]{2,1,0:T(8,128)(2,1)} %collective-permute-done.12), channel_id=1, source_target_pairs={{0,2},{2,0},{4,6},{6,4},{1,3},{3,1},{5,7},{7,5},{8,10},{10,8},{12,... | collective-permute-start | bytes 3145736 | tf_op jit(solution)/shard_map/ppermute | solution.py:10
  149.1 25.2 %collective-permute-start.15 = (bf16[512,1024]{1,0:T(8,128)(2,1)S(1)}, bf16[512,1024]{1,0:T(8,128)(2,1)}, u32[]{:S(2)}, u32[]{:S(2)}) collective-permute-start(bf16[512,1024]{1,0:T(8,128)(2,1)S(1)} %convolution_convert_fusion), channel_id=1, source_target_pairs={{0,1},{1,0},{2,3},{3,2},{4,5},{5,4},{6,7},{7,6},{8,9},{9,8},{10,11... | collective-permute-start | bytes 3145736 | tf_op jit(solution)/shard_map/ppermute | solution.py:10
  151.9 15.4 %collective-permute-start.5 = (bf16[1,272,1024]{2,1,0:T(8,128)(2,1)S(1)}, bf16[1,272,1024]{2,1,0:T(8,128)(2,1)S(1)}, u32[]{:S(2)}, u32[]{:S(2)}) collective-permute-start(bf16[1,272,1024]{2,1,0:T(8,128)(2,1)S(1)} %constant_dynamic-slice_fusion.9), channel_id=1, source_target_pairs={{0,8},{8,0},{16,24},{24,16},{1,9},{9,1},{17,25},{25,17},{2,10},{10... | collective-permute-start | bytes 1671176 | tf_op jit(solution)/shard_map/ppermute | solution.py:112
  169.8 37.2 %collective-permute-start.6 = (bf16[1,272,1024]{2,1,0:T(8,128)(2,1)}, bf16[1,272,1024]{2,1,0:T(8,128)(2,1)}, u32[]{:S(2)}, u32[]{:S(2)}) collective-permute-start(bf16[1,272,1024]{2,1,0:T(8,128)(2,1)} %get-tuple-element.17), channel_id=1, source_target_pairs={{0,16},{8,24},{16,0},{24,8},{1,17},{9,25},{17,1},{25,9},{2,18},{10... | collective-permute-start | bytes 1671176 | tf_op jit(solution)/shard_map/ppermute | solution.py:112
  171.0 49.2 %collective-permute-start.7 = (bf16[1,272,1024]{2,1,0:T(8,128)(2,1)}, bf16[1,272,1024]{2,1,0:T(8,128)(2,1)}, u32[]{:S(2)}, u32[]{:S(2)}) collective-permute-start(bf16[1,272,1024]{2,1,0:T(8,128)(2,1)} %get-tuple-element.16), channel_id=1, source_target_pairs={{0,24},{8,16},{16,8},{24,0},{1,25},{9,17},{17,9},{25,1},{2,26},{10... | collective-permute-start | bytes 1671176 | tf_op jit(solution)/shard_map/ppermute | solution.py:112
  175.6 5.6 %copy-start.4 = (bf16[512,1024]{1,0:T(8,128)(2,1)}, bf16[512,1024]{1,0:T(8,128)(2,1)S(1)}, u32[]{:S(2)}) copy-start(bf16[512,1024]{1,0:T(8,128)(2,1)S(1)} %get-tuple-element.23) | copy-start | bytes 3145732
  185.8 39.0 %copy-start.2 = (f32[1024,1024]{1,0:T(8,128)}, f32[1024,1024]{1,0:T(8,128)S(1)}, u32[]{:S(2)}) copy-start(f32[1024,1024]{1,0:T(8,128)S(1)} %fusion.9) | copy-start | bytes 12582916
  233.6 11.7 %copy-start.6 = (bf16[1024,1024]{1,0:T(8,128)(2,1)S(1)}, bf16[1024,1024]{1,0:T(8,128)(2,1)}, u32[]{:S(2)}) copy-start(bf16[1024,1024]{1,0:T(8,128)(2,1)} %get-tuple-element.15) | copy-start | bytes 6291460
  245.3 4.1 %copy-start.7 = (bf16[1024,1024]{1,0:T(8,128)(2,1)S(1)}, bf16[1024,1024]{1,0:T(8,128)(2,1)}, u32[]{:S(2)}) copy-start(bf16[1024,1024]{1,0:T(8,128)(2,1)} %get-tuple-element.15) | copy-start | bytes 6291460
  249.4 4.3 %copy-start.3 = (bf16[1024,1024]{1,0:T(8,128)(2,1)S(1)}, bf16[1024,1024]{1,0:T(8,128)(2,1)}, u32[]{:S(2)}) copy-start(bf16[1024,1024]{1,0:T(8,128)(2,1)} %get-tuple-element.14) | copy-start | bytes 6291460
  253.1 63.1 %collective-permute-start.16 = (bf16[1024,1024]{1,0:T(8,128)(2,1)}, bf16[1024,1024]{1,0:T(8,128)(2,1)}, u32[]{:S(2)}, u32[]{:S(2)}) collective-permute-start(bf16[1024,1024]{1,0:T(8,128)(2,1)} %fusion.24), channel_id=1, source_target_pairs={{0,1},{1,0},{2,3},{3,2},{4,5},{5,4},{6,7},{7,6},{8,9},{9,8},{10,11... | collective-permute-start | bytes 6291464 | tf_op jit(solution)/shard_map/ppermute | solution.py:10
  253.8 13.5 %collective-permute-start.17 = (bf16[1,256,1024]{2,1,0:T(8,128)(2,1)S(1)}, bf16[1,256,1024]{2,1,0:T(8,128)(2,1)S(1)}, u32[]{:S(2)}, u32[]{:S(2)}) collective-permute-start(bf16[1,256,1024]{2,1,0:T(8,128)(2,1)S(1)} %constant_dynamic-slice_fusion.6), channel_id=1, source_target_pairs={{0,8},{8,0},{16,24},{24,16},{1,9},{9,1},{17,25},{25,17},{2,10},{10... | collective-permute-start | bytes 1572872 | tf_op jit(solution)/shard_map/ppermute | solution.py:112
  268.4 33.4 %collective-permute-start.18 = (bf16[1,256,1024]{2,1,0:T(8,128)(2,1)}, bf16[1,256,1024]{2,1,0:T(8,128)(2,1)}, u32[]{:S(2)}, u32[]{:S(2)}) collective-permute-start(bf16[1,256,1024]{2,1,0:T(8,128)(2,1)} %get-tuple-element.20), channel_id=1, source_target_pairs={{0,16},{8,24},{16,0},{24,8},{1,17},{9,25},{17,1},{25,9},{2,18},{10... | collective-permute-start | bytes 1572872 | tf_op jit(solution)/shard_map/ppermute | solution.py:112
  268.4 46.7 %collective-permute-start.19 = (bf16[1,256,1024]{2,1,0:T(8,128)(2,1)}, bf16[1,256,1024]{2,1,0:T(8,128)(2,1)}, u32[]{:S(2)}, u32[]{:S(2)}) collective-permute-start(bf16[1,256,1024]{2,1,0:T(8,128)(2,1)} %get-tuple-element.19), channel_id=1, source_target_pairs={{0,24},{8,16},{16,8},{24,0},{1,25},{9,17},{17,9},{25,1},{2,26},{10... | collective-permute-start | bytes 1572872 | tf_op jit(solution)/shard_map/ppermute | solution.py:112
  326.3 4.4 %collective-permute-start.20 = (f32[8,128]{1,0:T(8,128)S(1)}, f32[8,128]{1,0:T(8,128)S(1)}, u32[]{:S(2)}, u32[]{:S(2)}) collective-permute-start(f32[8,128]{1,0:T(8,128)S(1)} %broadcast_in_dim.69), channel_id=1, source_target_pairs={{0,1},{1,0},{2,3},{3,2},{4,5},{5,4},{6,7},{7,6},{8,9},{9,8},{10,11... | collective-permute-start | bytes 12296 | tf_op jit(solution)/shard_map/ppermute | solution.py:10
  333.3 11.0 %copy-start.1 = (f32[4,1,256,1024]{3,2,1,0:T(8,128)S(1)}, f32[4,1,256,1024]{3,2,1,0:T(8,128)}, u32[]{:S(2)}) copy-start(f32[4,1,256,1024]{3,2,1,0:T(8,128)} %param.5) | copy-start | bytes 12582916
  335.3 7.1 %collective-permute-start.21 = (bf16[1,128,1024]{2,1,0:T(8,128)(2,1)S(1)}, bf16[1,128,1024]{2,1,0:T(8,128)(2,1)S(1)}, u32[]{:S(2)}, u32[]{:S(2)}) collective-permute-start(bf16[1,128,1024]{2,1,0:T(8,128)(2,1)S(1)} %constant_dynamic-slice_fusion.2), channel_id=1, source_target_pairs={{0,8},{8,0},{16,24},{24,16},{1,9},{9,1},{17,25},{25,17},{2,10},{10... | collective-permute-start | bytes 786440 | tf_op jit(solution)/shard_map/ppermute | solution.py:112
  342.5 18.0 %collective-permute-start.22 = (bf16[1,128,1024]{2,1,0:T(8,128)(2,1)S(1)}, bf16[1,128,1024]{2,1,0:T(8,128)(2,1)S(1)}, u32[]{:S(2)}, u32[]{:S(2)}) collective-permute-start(bf16[1,128,1024]{2,1,0:T(8,128)(2,1)S(1)} %get-tuple-element.25), channel_id=1, source_target_pairs={{0,16},{8,24},{16,0},{24,8},{1,17},{9,25},{17,1},{25,9},{2,18},{10... | collective-permute-start | bytes 786440 | tf_op jit(solution)/shard_map/ppermute | solution.py:112
  343.4 22.4 %collective-permute-start.23 = (bf16[1,128,1024]{2,1,0:T(8,128)(2,1)S(1)}, bf16[1,128,1024]{2,1,0:T(8,128)(2,1)S(1)}, u32[]{:S(2)}, u32[]{:S(2)}) collective-permute-start(bf16[1,128,1024]{2,1,0:T(8,128)(2,1)S(1)} %get-tuple-element.24), channel_id=1, source_target_pairs={{0,24},{8,16},{16,8},{24,0},{1,25},{9,17},{17,9},{25,1},{2,26},{10... | collective-permute-start | bytes 786440 | tf_op jit(solution)/shard_map/ppermute | solution.py:112
  365.8 1.0 copy-start.5
Sparse Core Ops, SparseCore 0:
  56.6 83.2 all-gather.1

commit v5 on v4

--- a/solution.py
+++ b/solution.py
@@ -1,6 +1,10 @@
+import functools
+
 import jax
 import jax.numpy as jnp
 from jax import lax
+from jax.experimental import pallas as pl
+from jax.experimental.pallas import tpu as pltpu
 from jax.sharding import PartitionSpec as P
 
 ITERS = 2
@@ -142,6 +146,60 @@
     return held
 
 
+def transfer_body(size, with_swap, *refs):
+    if with_swap:
+        pieces, whole, result, partner, send_sem, recv_sem, own_sem = refs
+    else:
+        pieces, result, send_sem, recv_sem, own_sem = refs
+    me = lax.axis_index("tok")
+    side = lax.axis_index("pair")
+    targets = [{"tok": lax.rem(me + step, size)} for step in range(1, size)]
+    if with_swap:
+        targets.append({"pair": 1 - side})
+    barrier = pltpu.get_barrier_semaphore()
+    for target in targets:
+        pl.semaphore_signal(barrier, inc=1, device_id=target, device_id_type=pl.DeviceIdType.MESH)
+    pl.semaphore_wait(barrier, len(targets))
+    copies = []
+    for slot, target in enumerate(targets):
+        to_pair = slot == size - 1
+        copies.append(
+            pltpu.make_async_remote_copy(
+                src_ref=whole if to_pair else pieces.at[target["tok"]],
+                dst_ref=partner if to_pair else result.at[me],
+                send_sem=send_sem.at[slot],
+                recv_sem=recv_sem.at[slot],
+                device_id=target,
+                device_id_type=pl.DeviceIdType.MESH,
+            )
+        )
+        copies[-1].start()
+    own = pltpu.make_async_copy(pieces.at[me], result.at[me], own_sem)
+    own.start()
+    own.wait()
+    for copy in copies:
+        copy.wait()
+
+
+def transfer(pieces, whole, collective_id):
+    size = lax.axis_size("tok")
+    arrays = [pieces] if whole is None else [pieces, whole]
+    slots = size - 1 + (whole is not None)
+    anywhere = pl.BlockSpec(memory_space=pl.ANY)
+    return pl.pallas_call(
+        functools.partial(transfer_body, size, whole is not None),
+        out_shape=[jax.ShapeDtypeStruct(array.shape, array.dtype) for array in arrays],
+        in_specs=[anywhere] * len(arrays),
+        out_specs=[anywhere] * len(arrays),
+        scratch_shapes=[
+            pltpu.SemaphoreType.DMA((slots,)),
+            pltpu.SemaphoreType.DMA((slots,)),
+            pltpu.SemaphoreType.DMA,
+        ],
+        compiler_params=pltpu.CompilerParams(collective_id=collective_id, has_side_effects=True),
+    )(*arrays)
+
+
 def owner_plan(inputs, output_grads, statistics):
     blocks, _, state_rows, order = statistics.shape
     tok_index = lax.axis_index("tok")
@@ -186,7 +244,7 @@
         factor_data, factor_data, (((1,), (1,)), ((), ())), preferred_element_type=jnp.float32
     )
     product = lax.optimization_barrier(product)
-    rows = exchange(product.astype(jnp.bfloat16).reshape(blocks, state_rows, order), "tok")
+    row_pieces = product.astype(jnp.bfloat16).reshape(blocks, state_rows, order)
     updated = 0.9 * previous + 0.1 * product
     identity = jnp.eye(order, dtype=jnp.float32)
     bound_max = jnp.max(jnp.sum(jnp.abs(updated), axis=1))
@@ -200,8 +258,7 @@
             square = dot_bf(factor, factor)
             fourth = dot_bf(square, square)
             iterate = lax.optimization_barrier(dot_bf(fourth, iterate))
-    partner = swapped(root, "pair", 0)
-    partner, rows = lax.optimization_barrier((partner, rows))
+    rows, partner = transfer(row_pieces, root, 0)
     left = jnp.where(first, root, partner)
     right = jnp.where(first, partner, root)
     left = left.reshape(blocks, 2, -1, order)
@@ -212,7 +269,7 @@
     update_sq = (local_sq + swapped(local_sq, "pair", 0))[0, 0]
     update = (raw * jnp.sqrt(grad_sq / (update_sq + 1e-06))).astype(jnp.bfloat16)
     new_rows = 0.9 * statistics + 0.1 * rows[:, None].astype(jnp.float32)
-    return (exchange(update.reshape(blocks, -1, order), "tok"), new_rows)
+    return (transfer(update.reshape(blocks, -1, order), None, 1)[0], new_rows)
 
 
 def per_device(inputs, output_grads, statistics):

time: 375 us -> 355 us (0.947)
  waiting for transfers between devices: 213 us -> 128 us
  Pallas kernels: 0 us -> 73.1 us
  starting transfers between devices: 30.4 us -> 25.4 us
    ppermute x9 -> x3, waiting for transfers between devices: 128 us -> 43 us  [exchange(): arrived = lax.ppermute(piece, axis, [(i, i ^ step) for i in range(size)])]
    pallas_call x0 -> x2, Pallas kernels: none -> 73.1 us  [transfer(): pl.pallas_call(functools.partial(transfer_body, size, whole is not None),...]
    unnamed x0 -> x1, other arithmetic: none -> 6.1 us
    ppermute x9 -> x3, starting transfers between devices: 9.94 us -> 6.32 us  [exchange(): arrived = lax.ppermute(piece, axis, [(i, i ^ step) for i in range(size)])]
    ppermute x11 -> x10, starting transfers between devices: 12.8 us -> 11.4 us  [swapped(): lax.ppermute(shard, axis, [(i, i ^ 1 << stride) for i in range(lax.axis_s...]
    ppermute x11 -> x10, waiting for transfers between devices: 33.3 us -> 33.2 us  [swapped(): lax.ppermute(shard, axis, [(i, i ^ 1 << stride) for i in range(lax.axis_s...]
  transfers between devices with their start and end apart: 25 -> 18, of which waited for: 16 -> 10; matrix products, arithmetic and copies ran while one was open for 15% -> 15% of each run, Pallas kernels for 0% -> 0%
where the time goes in v5:
time: 355 us; the launch traced here: 354 us
  waiting for transfers between devices  128 us (36%)
  Pallas kernels  73.1 us (21%)
  local copies, waits for them, and re-layouts  42.3 us (12%)
  matrix products  39.1 us (11%)
  other arithmetic  29.2 us (8%)
  starting transfers between devices  25.4 us (7%)
  between operations  16.9 us (5%)
    pallas_call x2, Pallas kernels, transfer(): pl.pallas_call(functools.partial(transfer_body, size, whole is not None),...  73.1 us
    ppermute x3, waiting for transfers between devices, exchange(): arrived = lax.ppermute(piece, axis, [(i, i ^ step) for i in range(size)])  43 us
    ppermute x10, waiting for transfers between devices, swapped(): lax.ppermute(shard, axis, [(i, i ^ 1 << stride) for i in range(lax.axis_s...  33.2 us
    ppermute x4, waiting for transfers between devices, cotangent_quarter(): arrived = lax.ppermute(piece, ('tok', 'tile'), pairs)  32.4 us
    all_gather x1, waiting for transfers between devices, owner_plan(): acts = lax.all_gather(acts, 'tok', axis=0, tiled=True)  19.8 us
    dot_general x3, matrix products, dot_bf(): jnp.dot(left_part, right_part, preferred_element_type=jnp.float32)  19.4 us
    dynamic_update_slice x8, local copies, waits for them, and re-layouts, owner_plan(): lax.dynamic_update_slice(cots, piece[:, None, None], (0, side, which, 0, 0))  14.5 us
    ppermute x10, starting transfers between devices, swapped(): lax.ppermute(shard, axis, [(i, i ^ 1 << stride) for i in range(lax.axis_s...  11.4 us
  transfers between devices with their start and end apart: 18, of which 10 were waited for; matrix products, arithmetic and copies ran while one was open for 15% of the time, Pallas kernels for 0%

profile of v5, /device:TPU:8, one launch (start us, length us, event | category | flops | bytes accessed | tf_op | source)
XLA Modules:
  0.0 354.5 jit_solution(7454357840462041039)
XLA Ops:
  7.3 1.3 constant_dynamic-slice_fusion.4
  8.5 1.9 collective-permute-start.1
  10.5 4.0 %collective-permute-start.2 = (bf16[1,128,1024]{2,1,0:T(8,128)(2,1)S(1)}, bf16[1,128,1024]{2,1,0:T(8,128)(2,1)}, u32[]{:S(2)}, u32[]{:S(2)}) collective-permute-start(bf16[1,128,1024]{2,1,0:T(8,128)(2,1)S(1)} %get-tuple-element.27), channel_id=1, source_target_pairs={{0,2},{2,10},{4,18},{6,26},{8,4},{10,12},{12,20},{14,28},{16,6},{1... | collective-permute-start | bytes 786440 | tf_op jit(solution)/shard_map/ppermute | solution.py:133
  14.5 1.3 constant_dynamic-slice_fusion.9
  15.7 1.6 collective-permute-start
  20.1 5.7 %collective-permute-done.2 = bf16[1,128,1024]{2,1,0:T(8,128)(2,1)} collective-permute-done((bf16[1,128,1024]{2,1,0:T(8,128)(2,1)S(1)}, bf16[1,128,1024]{2,1,0:T(8,128)(2,1)}, u32[]{:S(2)}, u32[]{:S(2)}) %collective-permute-start.2) | collective-permute-done | bytes 262176 | tf_op jit(solution)/shard_map/ppermute | solution.py:133
  26.7 26.7 %collective-permute-done.3 = bf16[1,128,1024]{2,1,0:T(8,128)(2,1)} collective-permute-done((bf16[1,128,1024]{2,1,0:T(8,128)(2,1)S(1)}, bf16[1,128,1024]{2,1,0:T(8,128)(2,1)}, u32[]{:S(2)}, u32[]{:S(2)}) %collective-permute-start.3) | collective-permute-done | bytes 262176 | tf_op jit(solution)/shard_map/ppermute | solution.py:133
  56.5 4.2 %collective-permute-start.8 = (bf16[4,128,1024]{2,1,0:T(8,128)(2,1)S(1)}, bf16[4,128,1024]{2,1,0:T(8,128)(2,1)}, u32[]{:S(2)}, u32[]{:S(2)}) collective-permute-start(bf16[4,128,1024]{2,1,0:T(8,128)(2,1)S(1)} %constant_dynamic-update-slice_fusion.3), channel_id=1, source_target_pairs={{0,4},{2,6},{4,0},{6,2},{1,5},{3,7},{5,1},{7,3},{8,12},{10,14},{12... | collective-permute-start | bytes 3145736 | tf_op jit(solution)/shard_map/ppermute | solution.py:14
  60.7 1.5 collective-permute-start.11
  62.4 2.7 bitcast_convert_fusion
  66.2 17.6 %collective-permute-done.8 = bf16[4,128,1024]{2,1,0:T(8,128)(2,1)} collective-permute-done((bf16[4,128,1024]{2,1,0:T(8,128)(2,1)S(1)}, bf16[4,128,1024]{2,1,0:T(8,128)(2,1)}, u32[]{:S(2)}, u32[]{:S(2)}) %collective-permute-start.8) | collective-permute-done | bytes 1048608 | tf_op jit(solution)/shard_map/ppermute | solution.py:14
  84.9 1.3 collective-permute-done.11
  86.5 1.6 pad_maximum_fusion
  88.0 4.3 %broadcast_in_dim.60 = bf16[4,2,4,128,1024]{4,3,2,1,0:T(8,128)(2,1)} broadcast(bf16[]{:T(256)} %constant.110.clone.1), dimensions={} | broadcast | bytes 8388610 | tf_op jit(solution)/shard_map/broadcast_in_dim | solution.py:215
  93.6 2.3 bitcast_dynamic-update-slice_fusion.5
  95.9 2.3 bitcast_dynamic-update-slice_fusion.4
  98.2 13.0 %collective-permute-done.12 = bf16[4,128,1024]{2,1,0:T(8,128)(2,1)} collective-permute-done((bf16[4,128,1024]{2,1,0:T(8,128)(2,1)}, bf16[4,128,1024]{2,1,0:T(8,128)(2,1)}, u32[]{:S(2)}, u32[]{:S(2)}) %collective-permute-start.12) | collective-permute-done | bytes 1048608 | tf_op jit(solution)/shard_map/ppermute | solution.py:14
  111.2 2.3 bitcast_dynamic-update-slice_fusion.3
  113.5 2.3 bitcast_dynamic-update-slice_fusion.2
  115.8 2.3 bitcast_dynamic-update-slice_fusion.1
  120.1 19.8 %all-gather.2.cloned.1.call-done = bf16[4096,512]{1,0:T(8,128)(2,1)} async-done(((bf16[1024,512]{1,0:T(8,128)(2,1)}), bf16[4096,512]{1,0:T(8,128)(2,1)}) %all-gather.2.cloned.1.call-update) | async-done | bytes 4194320 | tf_op jit(solution)/shard_map/all_gather | solution.py:214
  139.9 9.2 %convolution_convert_fusion = bf16[512,1024]{0,1:T(8,128)(2,1)S(1)} fusion(bf16[4096,512]{1,0:T(8,128)(2,1)} %all-gather.2.cloned.1.call-done, bf16[4096,1024]{1,0:T(8,128)(2,1)} %bitcast.18), kind=kOutput, calls=%fused_computation.40 | convolution fusion | flops 4295491584 | bytes 13631488 | tf_op jit(solution)/shard_map/dot_general | solution.py:234
  149.1 1.7 collective-permute-start.15
  151.9 3.1 collective-permute-start.5
  155.0 12.3 %collective-permute-done.5 = bf16[1,272,1024]{2,1,0:T(8,128)(2,1)S(1)} collective-permute-done((bf16[1,272,1024]{2,1,0:T(8,128)(2,1)S(1)}, bf16[1,272,1024]{2,1,0:T(8,128)(2,1)S(1)}, u32[]{:S(2)}, u32[]{:S(2)}) %collective-permute-start.5) | collective-permute-done | bytes 557088 | tf_op jit(solution)/shard_map/ppermute | solution.py:116
  167.3 2.5 constant_dynamic-slice_fusion.1
  169.8 1.3 collective-permute-start.6
  171.1 1.9 collective-permute-start.7
  174.3 1.4 broadcast_select_fusion.2
  175.7 1.7 pad_maximum_fusion.1
  177.3 4.0 %copy.17 = bf16[1024,1024]{1,0:T(8,128)(2,1)} copy(bf16[1024,1024]{0,1:T(8,128)(2,1)} %pad_maximum_fusion.1) | data formatting | bytes 4194304 | tf_op jit(solution)/shard_map/concatenate | solution.py:239
  181.3 4.6 %fusion.10 = f32[1024,1024]{1,0:T(8,128)S(1)} fusion(bf16[1024,1024]{1,0:T(8,128)(2,1)} %copy.17, pred[]{:T(512)S(6)} %eq.39, bf16[512,1024]{0,1:T(8,128)(2,1)S(1)} %get-tuple-element.24, bf16[512,1024]{0,1:T(8,128)(2,1)S(1)} %get-tuple-element.23), kind=kOutput, calls=%fused_computation.23 | convolution fusion | flops 2152726528 | bytes 8388609 | tf_op jit(solution)/shard_map/dot_general | solution.py:243
  185.9 1.9 multiply_reduce_fusion
  187.8 19.3 %collective-permute-done.6 = bf16[1,272,1024]{2,1,0:T(8,128)(2,1)} collective-permute-done((bf16[1,272,1024]{2,1,0:T(8,128)(2,1)}, bf16[1,272,1024]{2,1,0:T(8,128)(2,1)}, u32[]{:S(2)}, u32[]{:S(2)}) %collective-permute-start.6) | collective-permute-done | bytes 557088 | tf_op jit(solution)/shard_map/ppermute | solution.py:116
  207.1 1.9 constant_dynamic-update-slice_fusion.1
  209.0 11.4 %collective-permute-done.7 = bf16[1,272,1024]{2,1,0:T(8,128)(2,1)} collective-permute-done((bf16[1,272,1024]{2,1,0:T(8,128)(2,1)}, bf16[1,272,1024]{2,1,0:T(8,128)(2,1)}, u32[]{:S(2)}, u32[]{:S(2)}) %collective-permute-start.7) | collective-permute-done | bytes 557088 | tf_op jit(solution)/shard_map/ppermute | solution.py:116
  220.4 1.9 constant_dynamic-update-slice_fusion
  222.3 1.8 slice.12
  227.9 5.8 %divide_convert_fusion = (bf16[1024,1024]{1,0:T(8,128)(2,1)}, bf16[1024,1024]{1,0:T(8,128)(2,1)}) fusion(f32[]{:T(128)S(6)} %mul_shard_map.3, f32[]{:T(128)S(6)} %mul.81, f32[1024,1024]{1,0:T(8,128)} %copy-done.1, f32[1024]{0:T(1024)S(1)} %fusion.36, bf16[4,256,1024]{2,1,0:T(8,128)(2,1)S(1)} %slice.12), kind=kLoop, calls=%fused_computation.16 | loop fusion | flops 12582912 | bytes 10489864 | tf_op jit(solution)/shard_map/convert_element_type | solution.py:251
  233.7 11.8 %fusion.15 = bf16[1024,1024]{1,0:T(8,128)(2,1)} fusion(bf16[1024,1024]{1,0:T(8,128)(2,1)} %get-tuple-element.18), kind=kOutput, calls=%fused_computation.30 | convolution fusion | flops 4302307328 | bytes 4194304 | tf_op jit(solution)/shard_map/dot_general | solution.py:107
  245.5 3.9 %fusion.22 = bf16[1024,1024]{1,0:T(8,128)(2,1)S(1)} fusion(bf16[1024,1024]{1,0:T(8,128)(2,1)S(1)} %copy-done.4, bf16[1024,1024]{1,0:T(8,128)(2,1)} %fusion.15), kind=kOutput, calls=%fused_computation.38 | convolution fusion | flops 2148532224 | bytes 6291456 | tf_op jit(solution)/shard_map/dot_general | solution.py:107
  249.4 3.7 %fusion.25.refs_1_ = bf16[1024,1024]{1,0:T(8,128)(2,1)} fusion(bf16[1024,1024]{1,0:T(8,128)(2,1)S(1)} %fusion.22, bf16[1024,1024]{1,0:T(8,128)(2,1)S(1)} %copy-done.4), kind=kOutput, calls=%fused_computation.39 | convolution fusion | flops 2161115136 | bytes 6291456 | tf_op jit(solution)/shard_map/dot_general | solution.py:107
  253.1 48.0 %shard_map.50 = (bf16[4,256,1024]{2,1,0:T(8,128)(2,1)}, bf16[1024,1024]{1,0:T(8,128)(2,1)}) custom-call(bf16[4,256,1024]{2,1,0:T(8,128)(2,1)} %bitcast.67, bf16[1024,1024]{1,0:T(8,128)(2,1)} %fusion.25.refs_1_), custom_call_target="tpu_custom_call" | custom-call | tf_op jit(solution)/shard_map/pallas_call | solution.py:189
  301.1 1.9 broadcast_select_fusion
  303.1 5.9 %multiply_reduce_fusion.1 = (f32[]{:T(128)}, f32[512,1024]{1,0:T(8,128)}) fusion(bf16[1024,1024]{1,0:T(8,128)(2,1)} %get-tuple-element.12, bf16[1024,1024]{1,0:T(8,128)(2,1)} %fusion.25.refs_1_, pred[]{:T(512)S(6)} %eq.39, bf16[512,1024]{1,0:T(8,128)(2,1)S(1)} %bitcast.71, bf16[512,1024]{0,1:T(8,128)(2,1)S(1)} %copy-done.3, ...), kind=kOutput, calls=%fused_computation.25 | convolution fusion | flops 2154299392 | bytes 9437189 | tf_op jit(solution)/shard_map/dot_general | solution.py:267
  310.3 6.1 %fusion.6 = f32[4,1,256,1024]{3,2,1,0:T(8,128)} fusion(f32[4,1,256,1024]{3,2,1,0:T(8,128)} %param.5, bf16[4,256,1024]{2,1,0:T(8,128)(2,1)} %get-tuple-element.13), kind=kLoop, calls=%fused_computation.10 | loop fusion | flops 4194304 | bytes 10485760
  320.2 25.2 %shard_map.51 = bf16[4,128,1024]{2,1,0:T(8,128)(2,1)} custom-call(bf16[4,128,1024]{2,1,0:T(8,128)(2,1)} %bitcast.69), custom_call_target="tpu_custom_call" | custom-call | tf_op jit(solution)/shard_map/pallas_call | solution.py:189
  345.3 2.3 copy.37
  (54 shorter events, 21.6 us)
Async XLA Ops:
  7.2 132.7 %all-gather.2.cloned.1.call-start = ((), (), s32[]{:S(2)}) async-start(), calls=%async_computation | async-start | bytes 5242880 | tf_op jit(solution)/shard_map/all_gather | solution.py:214
  8.5 10.4 %collective-permute-start.1 = (bf16[1,128,1024]{2,1,0:T(8,128)(2,1)S(1)}, bf16[1,128,1024]{2,1,0:T(8,128)(2,1)}, u32[]{:S(2)}, u32[]{:S(2)}) collective-permute-start(bf16[1,128,1024]{2,1,0:T(8,128)(2,1)S(1)} %get-tuple-element.28), channel_id=1, source_target_pairs={{0,0},{2,8},{4,16},{6,24},{8,2},{10,10},{12,18},{14,26},{16,4},{18... | collective-permute-start | bytes 786440 | tf_op jit(solution)/shard_map/ppermute | solution.py:133
  10.5 15.3 %collective-permute-start.2 = (bf16[1,128,1024]{2,1,0:T(8,128)(2,1)S(1)}, bf16[1,128,1024]{2,1,0:T(8,128)(2,1)}, u32[]{:S(2)}, u32[]{:S(2)}) collective-permute-start(bf16[1,128,1024]{2,1,0:T(8,128)(2,1)S(1)} %get-tuple-element.27), channel_id=1, source_target_pairs={{0,2},{2,10},{4,18},{6,26},{8,4},{10,12},{12,20},{14,28},{16,6},{1... | collective-permute-start | bytes 786440 | tf_op jit(solution)/shard_map/ppermute | solution.py:133
  15.7 39.7 %collective-permute-start = (bf16[512,512]{1,0:T(8,128)(2,1)S(1)}, bf16[512,512]{1,0:T(8,128)(2,1)S(1)}, u32[]{:S(2)}, u32[]{:S(2)}) collective-permute-start(bf16[512,512]{1,0:T(8,128)(2,1)S(1)} %get-tuple-element.30), channel_id=1, source_target_pairs={{0,1},{1,0},{2,3},{3,2},{4,5},{5,4},{6,7},{7,6},{8,9},{9,8},{10,11... | collective-permute-start | bytes 1572872 | tf_op jit(solution)/shard_map/ppermute | solution.py:14
  17.3 36.2 %collective-permute-start.3 = (bf16[1,128,1024]{2,1,0:T(8,128)(2,1)S(1)}, bf16[1,128,1024]{2,1,0:T(8,128)(2,1)}, u32[]{:S(2)}, u32[]{:S(2)}) collective-permute-start(bf16[1,128,1024]{2,1,0:T(8,128)(2,1)S(1)} %get-tuple-element.26), channel_id=1, source_target_pairs={{0,4},{2,12},{4,20},{6,28},{8,6},{10,14},{12,22},{14,30},{16,0},{1... | collective-permute-start | bytes 786440 | tf_op jit(solution)/shard_map/ppermute | solution.py:133
  18.2 36.2 %collective-permute-start.4 = (bf16[1,128,1024]{2,1,0:T(8,128)(2,1)S(1)}, bf16[1,128,1024]{2,1,0:T(8,128)(2,1)}, u32[]{:S(2)}, u32[]{:S(2)}) collective-permute-start(bf16[1,128,1024]{2,1,0:T(8,128)(2,1)S(1)} %get-tuple-element.25), channel_id=1, source_target_pairs={{0,6},{2,14},{4,22},{6,30},{8,0},{10,8},{12,16},{14,24},{16,2},{18... | collective-permute-start | bytes 786440 | tf_op jit(solution)/shard_map/ppermute | solution.py:133
  56.5 27.4 %collective-permute-start.8 = (bf16[4,128,1024]{2,1,0:T(8,128)(2,1)S(1)}, bf16[4,128,1024]{2,1,0:T(8,128)(2,1)}, u32[]{:S(2)}, u32[]{:S(2)}) collective-permute-start(bf16[4,128,1024]{2,1,0:T(8,128)(2,1)S(1)} %constant_dynamic-update-slice_fusion.3), channel_id=1, source_target_pairs={{0,4},{2,6},{4,0},{6,2},{1,5},{3,7},{5,1},{7,3},{8,12},{10,14},{12... | collective-permute-start | bytes 3145736 | tf_op jit(solution)/shard_map/ppermute | solution.py:14
  60.7 25.6 %collective-permute-start.11 = (bf16[4,128,1024]{2,1,0:T(8,128)(2,1)S(1)}, bf16[4,128,1024]{2,1,0:T(8,128)(2,1)}, u32[]{:S(2)}, u32[]{:S(2)}) collective-permute-start(bf16[4,128,1024]{2,1,0:T(8,128)(2,1)S(1)} %constant_dynamic-update-slice_fusion.3), channel_id=1, source_target_pairs={{0,1},{1,0},{2,3},{3,2},{4,5},{5,4},{6,7},{7,6},{8,9},{9,8},{10,11... | collective-permute-start | bytes 3145736 | tf_op jit(solution)/shard_map/ppermute | solution.py:14
  62.2 3.4 copy-start
  65.1 30.8 %collective-permute-start.9 = (bf16[4,128,1024]{2,1,0:T(8,128)(2,1)S(1)}, bf16[4,128,1024]{2,1,0:T(8,128)(2,1)}, u32[]{:S(2)}, u32[]{:S(2)}) collective-permute-start(bf16[4,128,1024]{2,1,0:T(8,128)(2,1)S(1)} %constant_dynamic-update-slice_fusion.3), channel_id=1, source_target_pairs={{0,2},{2,0},{4,6},{6,4},{1,3},{3,1},{5,7},{7,5},{8,10},{10,8},{12,... | collective-permute-start | bytes 3145736 | tf_op jit(solution)/shard_map/ppermute | solution.py:14
  83.9 27.3 %collective-permute-start.10 = (bf16[4,128,1024]{2,1,0:T(8,128)(2,1)}, bf16[4,128,1024]{2,1,0:T(8,128)(2,1)}, u32[]{:S(2)}, u32[]{:S(2)}) collective-permute-start(bf16[4,128,1024]{2,1,0:T(8,128)(2,1)} %collective-permute-done.8), channel_id=1, source_target_pairs={{0,2},{2,0},{4,6},{6,4},{1,3},{3,1},{5,7},{7,5},{8,10},{10,8},{12,... | collective-permute-start | bytes 3145736 | tf_op jit(solution)/shard_map/ppermute | solution.py:14
  86.2 24.9 %collective-permute-start.12 = (bf16[4,128,1024]{2,1,0:T(8,128)(2,1)}, bf16[4,128,1024]{2,1,0:T(8,128)(2,1)}, u32[]{:S(2)}, u32[]{:S(2)}) collective-permute-start(bf16[4,128,1024]{2,1,0:T(8,128)(2,1)} %collective-permute-done.11), channel_id=1, source_target_pairs={{0,4},{2,6},{4,0},{6,2},{1,5},{3,7},{5,1},{7,3},{8,12},{10,14},{12... | collective-permute-start | bytes 3145736 | tf_op jit(solution)/shard_map/ppermute | solution.py:14
  93.3 24.7 %collective-permute-start.13 = (bf16[4,128,1024]{2,1,0:T(8,128)(2,1)}, bf16[4,128,1024]{2,1,0:T(8,128)(2,1)S(1)}, u32[]{:S(2)}, u32[]{:S(2)}) collective-permute-start(bf16[4,128,1024]{2,1,0:T(8,128)(2,1)} %collective-permute-done.11), channel_id=1, source_target_pairs={{0,2},{2,0},{4,6},{6,4},{1,3},{3,1},{5,7},{7,5},{8,10},{10,8},{12,... | collective-permute-start | bytes 3145736 | tf_op jit(solution)/shard_map/ppermute | solution.py:14
  111.2 7.9 %collective-permute-start.14 = (bf16[4,128,1024]{2,1,0:T(8,128)(2,1)}, bf16[4,128,1024]{2,1,0:T(8,128)(2,1)S(1)}, u32[]{:S(2)}, u32[]{:S(2)}) collective-permute-start(bf16[4,128,1024]{2,1,0:T(8,128)(2,1)} %collective-permute-done.12), channel_id=1, source_target_pairs={{0,2},{2,0},{4,6},{6,4},{1,3},{3,1},{5,7},{7,5},{8,10},{10,8},{12,... | collective-permute-start | bytes 3145736 | tf_op jit(solution)/shard_map/ppermute | solution.py:14
  149.1 25.2 %collective-permute-start.15 = (bf16[512,1024]{0,1:T(8,128)(2,1)S(1)}, bf16[512,1024]{0,1:T(8,128)(2,1)}, u32[]{:S(2)}, u32[]{:S(2)}) collective-permute-start(bf16[512,1024]{0,1:T(8,128)(2,1)S(1)} %convolution_convert_fusion), channel_id=1, source_target_pairs={{0,1},{1,0},{2,3},{3,2},{4,5},{5,4},{6,7},{7,6},{8,9},{9,8},{10,11... | collective-permute-start | bytes 3145736 | tf_op jit(solution)/shard_map/ppermute | solution.py:14
  151.9 15.4 %collective-permute-start.5 = (bf16[1,272,1024]{2,1,0:T(8,128)(2,1)S(1)}, bf16[1,272,1024]{2,1,0:T(8,128)(2,1)S(1)}, u32[]{:S(2)}, u32[]{:S(2)}) collective-permute-start(bf16[1,272,1024]{2,1,0:T(8,128)(2,1)S(1)} %constant_dynamic-slice_fusion.3), channel_id=1, source_target_pairs={{0,8},{8,0},{16,24},{24,16},{1,9},{9,1},{17,25},{25,17},{2,10},{10... | collective-permute-start | bytes 1671176 | tf_op jit(solution)/shard_map/ppermute | solution.py:116
  169.8 37.3 %collective-permute-start.6 = (bf16[1,272,1024]{2,1,0:T(8,128)(2,1)}, bf16[1,272,1024]{2,1,0:T(8,128)(2,1)}, u32[]{:S(2)}, u32[]{:S(2)}) collective-permute-start(bf16[1,272,1024]{2,1,0:T(8,128)(2,1)} %get-tuple-element.21), channel_id=1, source_target_pairs={{0,16},{8,24},{16,0},{24,8},{1,17},{9,25},{17,1},{25,9},{2,18},{10... | collective-permute-start | bytes 1671176 | tf_op jit(solution)/shard_map/ppermute | solution.py:116
  171.1 49.3 %collective-permute-start.7 = (bf16[1,272,1024]{2,1,0:T(8,128)(2,1)}, bf16[1,272,1024]{2,1,0:T(8,128)(2,1)}, u32[]{:S(2)}, u32[]{:S(2)}) collective-permute-start(bf16[1,272,1024]{2,1,0:T(8,128)(2,1)} %get-tuple-element.20), channel_id=1, source_target_pairs={{0,24},{8,16},{16,8},{24,0},{1,25},{9,17},{17,9},{25,1},{2,26},{10... | collective-permute-start | bytes 1671176 | tf_op jit(solution)/shard_map/ppermute | solution.py:116
  175.6 10.2 %copy-start.2 = (bf16[512,1024]{0,1:T(8,128)(2,1)}, bf16[512,1024]{0,1:T(8,128)(2,1)S(1)}, u32[]{:S(2)}) copy-start(bf16[512,1024]{0,1:T(8,128)(2,1)S(1)} %get-tuple-element.24) | copy-start | bytes 3145732
  185.9 39.0 %copy-start.1 = (f32[1024,1024]{1,0:T(8,128)}, f32[1024,1024]{1,0:T(8,128)S(1)}, u32[]{:S(2)}) copy-start(f32[1024,1024]{1,0:T(8,128)S(1)} %fusion.10) | copy-start | bytes 12582916
  233.7 11.8 %copy-start.4 = (bf16[1024,1024]{1,0:T(8,128)(2,1)S(1)}, bf16[1024,1024]{1,0:T(8,128)(2,1)}, u32[]{:S(2)}) copy-start(bf16[1024,1024]{1,0:T(8,128)(2,1)} %get-tuple-element.18) | copy-start | bytes 6291460
  301.1 2.0 copy-start.3
  309.7 6.8 %collective-permute-start.16 = (f32[8,128]{1,0:T(8,128)S(1)}, f32[8,128]{1,0:T(8,128)S(1)}, u32[]{:S(2)}, u32[]{:S(2)}) collective-permute-start(f32[8,128]{1,0:T(8,128)S(1)} %broadcast_in_dim.69), channel_id=1, source_target_pairs={{0,1},{1,0},{2,3},{3,2},{4,5},{5,4},{6,7},{7,6},{8,9},{9,8},{10,11... | collective-permute-start | bytes 12296 | tf_op jit(solution)/shard_map/ppermute | solution.py:14
  310.3 8.6 %copy-start.5 = (f32[512,1024]{1,0:T(8,128)S(1)}, f32[512,1024]{1,0:T(8,128)}, u32[]{:S(2)}) copy-start(f32[512,1024]{1,0:T(8,128)} %get-tuple-element.32) | copy-start | bytes 6291460
Sparse Core Ops, SparseCore 0:
  56.6 83.2 all-gather.1
